TPU v7x, 512 devices: a whole 4x8x8 slice. The times are simulated.
512 devices in a mesh: head: 8 (over x, y_lo), ctx: 64 (over z, y_hi, core).
Axes of the slice: x: 4, y: 8 (y_hi: 4, y_lo: 2; y = y_hi * 2 + y_lo), z: 8, core: 2. Of those that a mesh axis runs over, the one named last changes fastest.
Arguments:
- query_states: bfloat16 [65536, 32, 128], P(('ctx', 'head')), may hold values from -6 to 6
- key_states: bfloat16 [65536, 4, 128], P(('ctx', 'head')), may hold values from -6 to 6
- value_states: bfloat16 [65536, 4, 128], P(('ctx', 'head')), may hold values from -6 to 6
- out_grad: bfloat16 [65536, 32, 128], P(('ctx', 'head')), may hold values from -6 to 6
- log_norm: float32 [65536, 32], P(('ctx', 'head')), may hold values from 4 to 7
- row_delta: float32 [65536, 32], P(('ctx', 'head')), may hold values from -6 to 6
- doc_lengths: int32 [256], replicated, may hold values from 1 to 512, 65536 in all
Outputs:
- query_grad: bfloat16 [65536, 32, 128], P(('ctx', 'head'))
- key_grad: bfloat16 [65536, 4, 128], P(('ctx', 'head'))
- value_grad: bfloat16 [65536, 4, 128], P(('ctx', 'head'))
Inputs may be any that keep to these rules, and one draw needn't show every extreme that they name: `doc_lengths`: documents lie end to end in the pack, in order; their lengths sum to 65536 and the longest is exactly 512.
All inputs are finite; a program needn't handle non-finite values.
Results may differ from a plain program's by a relative error of at most 0.012.
Values may be sent and summed in bfloat16 or wider, within the bound.
No kernel may reach another device: no remote copies, remote signals or barrier semaphores. Data moves between devices by JAX's collectives and lax.ppermute only.
A program may use at most 64 MiB of HBM per device.

v0:
```python
import math

import jax
import jax.numpy as jnp
from jax import lax
from jax.sharding import PartitionSpec as P

KV_HEADS = 4
HEAD_DIM = 128


def shifted(x, axis, by):
    count = lax.axis_size(axis)
    pairs = [(i, i + by) for i in range(count) if 0 <= i + by < count]
    return lax.ppermute(x, axis, pairs)


def doc_starts(doc_lengths, positions):
    doc_ends = jnp.cumsum(doc_lengths)
    before = jnp.where(doc_ends[None, :] <= positions[:, None], doc_lengths[None, :], 0)
    return jnp.sum(before, axis=1)


def across_rows(left, right):
    return lax.dot_general(
        left, right, (((0,), (0,)), ((), ())), preferred_element_type=jnp.float32
    )


def across_cols(left, right):
    return lax.dot_general(
        left, right, (((1,), (1,)), ((), ())), preferred_element_type=jnp.float32
    )


def tile_terms(
    query_rows, grad_rows, norm_rows, delta_rows, key_cols, value_cols, allowed, softmax_scale
):
    scores = across_cols(query_rows, key_cols) * softmax_scale
    attn_prob = jnp.where(allowed, jnp.exp(scores - norm_rows[:, None]), 0.0)
    prob_grad = across_cols(grad_rows, value_cols)
    score_grad = (attn_prob * (prob_grad - delta_rows[:, None])).astype(jnp.bfloat16)
    prob_low = attn_prob.astype(jnp.bfloat16)
    query_part = jnp.dot(score_grad, key_cols, preferred_element_type=jnp.float32) * softmax_scale
    key_part = across_rows(score_grad, query_rows) * softmax_scale
    value_part = across_rows(prob_low, grad_rows)
    return (query_part, key_part, value_part)


def shift_rim(rim_keys, rim_values):
    return shifted((rim_keys, rim_values), "ctx", 1)


def shards(query_states, key_states, value_states, out_grad, log_norm, row_delta, doc_lengths):
    head_count = lax.axis_size("head")
    shard_rows = query_states.shape[0] * head_count
    rim_rows = min(512, shard_rows)
    head_local = query_states.shape[1] // head_count
    copies = max(1, head_count // KV_HEADS)
    softmax_scale = 1.0 / math.sqrt(HEAD_DIM)
    tail_start = shard_rows - rim_rows
    key_copies = jnp.repeat(key_states, copies, axis=1)
    value_copies = jnp.repeat(value_states, copies, axis=1)
    query_local, grad_local, key_local, value_local = (
        lax.all_to_all(query_states, "head", split_axis=1, concat_axis=0, tiled=True),
        lax.all_to_all(out_grad, "head", split_axis=1, concat_axis=0, tiled=True),
        lax.all_to_all(key_copies, "head", split_axis=1, concat_axis=0, tiled=True),
        lax.all_to_all(value_copies, "head", split_axis=1, concat_axis=0, tiled=True),
    )
    rim_keys, rim_values = shift_rim(key_local[tail_start:], value_local[tail_start:])
    norm_local, delta_local = (
        lax.all_to_all(log_norm, "head", split_axis=1, concat_axis=0, tiled=True),
        lax.all_to_all(row_delta, "head", split_axis=1, concat_axis=0, tiled=True),
    )
    key_ext = jnp.concatenate([rim_keys, key_local], axis=0)
    value_ext = jnp.concatenate([rim_values, value_local], axis=0)
    kv_local = key_ext.shape[1]
    heads_per_kv = head_local // kv_local
    first_pos = lax.axis_index("ctx") * shard_rows
    query_pos = first_pos + jnp.arange(shard_rows, dtype=jnp.int32)
    starts = doc_starts(doc_lengths, query_pos)
    block_count = shard_rows // rim_rows
    window = 2 * rim_rows

    def block_head(counter, totals):
        query_total, key_total, value_total = totals
        head_index = counter // block_count
        first_row = counter % block_count * rim_rows
        kv_index = head_index // heads_per_kv
        query_rows = lax.dynamic_slice(
            query_local, (first_row, head_index, 0), (rim_rows, 1, HEAD_DIM)
        ).reshape(rim_rows, HEAD_DIM)
        grad_rows = lax.dynamic_slice(
            grad_local, (first_row, head_index, 0), (rim_rows, 1, HEAD_DIM)
        ).reshape(rim_rows, HEAD_DIM)
        norm_rows = lax.dynamic_slice(norm_local, (first_row, head_index), (rim_rows, 1)).reshape(
            rim_rows
        )
        delta_rows = lax.dynamic_slice(delta_local, (first_row, head_index), (rim_rows, 1)).reshape(
            rim_rows
        )
        key_cols = lax.dynamic_slice(
            key_ext, (first_row, kv_index, 0), (window, 1, HEAD_DIM)
        ).reshape(window, HEAD_DIM)
        value_cols = lax.dynamic_slice(
            value_ext, (first_row, kv_index, 0), (window, 1, HEAD_DIM)
        ).reshape(window, HEAD_DIM)
        row_pos = first_pos + first_row + jnp.arange(rim_rows, dtype=jnp.int32)
        col_pos = first_pos + first_row - rim_rows + jnp.arange(window, dtype=jnp.int32)
        row_starts = lax.dynamic_slice_in_dim(starts, first_row, rim_rows)
        allowed = (col_pos[None, :] <= row_pos[:, None]) & (col_pos[None, :] >= row_starts[:, None])
        query_part, key_part, value_part = tile_terms(
            query_rows,
            grad_rows,
            norm_rows,
            delta_rows,
            key_cols,
            value_cols,
            allowed,
            softmax_scale,
        )
        query_total = lax.dynamic_update_slice(
            query_total,
            query_part.astype(jnp.bfloat16).reshape(rim_rows, 1, HEAD_DIM),
            (first_row, head_index, 0),
        )
        key_window = lax.dynamic_slice(key_total, (first_row, kv_index, 0), (window, 1, HEAD_DIM))
        value_window = lax.dynamic_slice(
            value_total, (first_row, kv_index, 0), (window, 1, HEAD_DIM)
        )
        key_total = lax.dynamic_update_slice(
            key_total, key_window + key_part.reshape(window, 1, HEAD_DIM), (first_row, kv_index, 0)
        )
        value_total = lax.dynamic_update_slice(
            value_total,
            value_window + value_part.reshape(window, 1, HEAD_DIM),
            (first_row, kv_index, 0),
        )
        return (query_total, key_total, value_total)

    start_totals = (
        jnp.zeros((shard_rows, head_local, HEAD_DIM), jnp.bfloat16),
        jnp.zeros((rim_rows + shard_rows, kv_local, HEAD_DIM), jnp.float32),
        jnp.zeros((rim_rows + shard_rows, kv_local, HEAD_DIM), jnp.float32),
    )
    query_total, key_total, value_total = lax.fori_loop(
        0, block_count * head_local, block_head, start_totals
    )
    back_keys, back_values = shifted((key_total[:rim_rows], value_total[:rim_rows]), "ctx", -1)
    key_own = jnp.concatenate(
        [key_total[rim_rows:shard_rows], key_total[shard_rows:] + back_keys], axis=0
    )
    value_own = jnp.concatenate(
        [value_total[rim_rows:shard_rows], value_total[shard_rows:] + back_values], axis=0
    )
    query_grad = lax.all_to_all(query_total, "head", split_axis=0, concat_axis=1, tiled=True)
    key_parts, value_parts = (
        lax.all_to_all(
            key_own.astype(jnp.bfloat16), "head", split_axis=0, concat_axis=1, tiled=True
        ).astype(key_own.dtype),
        lax.all_to_all(
            value_own.astype(jnp.bfloat16), "head", split_axis=0, concat_axis=1, tiled=True
        ).astype(value_own.dtype),
    )
    tok_rows = key_parts.shape[0]
    key_grad = jnp.sum(key_parts.reshape(tok_rows, KV_HEADS, copies, HEAD_DIM), axis=2).astype(
        jnp.bfloat16
    )
    value_grad = jnp.sum(value_parts.reshape(tok_rows, KV_HEADS, copies, HEAD_DIM), axis=2).astype(
        jnp.bfloat16
    )
    return (query_grad, key_grad, value_grad)


def solution(mesh):
    return jax.shard_map(
        shards,
        mesh=mesh,
        in_specs=(
            P(("ctx", "head"), None, None),
            P(("ctx", "head"), None, None),
            P(("ctx", "head"), None, None),
            P(("ctx", "head"), None, None),
            P(("ctx", "head"), None),
            P(("ctx", "head"), None),
            P(),
        ),
        out_specs=(
            P(("ctx", "head"), None, None),
            P(("ctx", "head"), None, None),
            P(("ctx", "head"), None, None),
        ),
        check_vma=False,
    )
```

profile of v0, /device:TPU:256, one launch (start us, length us, event | category | flops | bytes accessed | tf_op | source)
XLA Modules:
  0.0 182.4 jit_solution(973606999725791476)
XLA Ops:
  0.6 5.5 %all-to-all-start.2 = ((f32[128,8,4]{0,2,1:T(4,128)}), f32[128,8,4]{0,2,1:T(4,128)S(1)}, u32[]{:S(2)}, u32[]{:S(2)}) async-start(f32[128,8,4]{0,2,1:T(4,128)} %bitcast.131), calls=%async_computation.2 | async-start | bytes 32768 | tf_op jit(solution)/shard_map/all_to_all | solution.py:72
  7.0 5.3 %all-to-all-done.2 = f32[128,8,4]{0,2,1:T(4,128)S(1)} async-done(((f32[128,8,4]{0,2,1:T(4,128)}), f32[128,8,4]{0,2,1:T(4,128)S(1)}, u32[]{:S(2)}, u32[]{:S(2)}) %all-to-all-start.2) | async-done | bytes 16416 | tf_op jit(solution)/shard_map/all_to_all | solution.py:72
  13.0 3.4 %all-to-all-start.1 = ((bf16[128,8,128]{2,0,1:T(8,128)(2,1)}), bf16[128,8,128]{2,0,1:T(8,128)(2,1)S(1)}, u32[]{:S(2)}, u32[]{:S(2)}) async-start(bf16[128,8,128]{2,0,1:T(8,128)(2,1)} %bitcast.14), calls=%async_computation.1 | async-start | bytes 524288 | tf_op jit(solution)/shard_map/all_to_all | solution.py:67
  17.4 6.3 %all-to-all-done.1 = bf16[128,8,128]{2,0,1:T(8,128)(2,1)S(1)} async-done(((bf16[128,8,128]{2,0,1:T(8,128)(2,1)}), bf16[128,8,128]{2,0,1:T(8,128)(2,1)S(1)}, u32[]{:S(2)}, u32[]{:S(2)}) %all-to-all-start.1) | async-done | bytes 262176 | tf_op jit(solution)/shard_map/all_to_all | solution.py:67
  24.4 3.4 %all-to-all-start.4 = ((bf16[128,8,128]{2,0,1:T(8,128)(2,1)}), bf16[128,8,128]{2,0,1:T(8,128)(2,1)S(1)}, u32[]{:S(2)}, u32[]{:S(2)}) async-start(bf16[128,8,128]{2,0,1:T(8,128)(2,1)} %bitcast.26), calls=%async_computation.4 | async-start | bytes 524288 | tf_op jit(solution)/shard_map/all_to_all | solution.py:68
  27.9 1.4 copy.72
  29.2 5.8 %all-to-all-done.4 = bf16[128,8,128]{2,0,1:T(8,128)(2,1)S(1)} async-done(((bf16[128,8,128]{2,0,1:T(8,128)(2,1)}), bf16[128,8,128]{2,0,1:T(8,128)(2,1)S(1)}, u32[]{:S(2)}, u32[]{:S(2)}) %all-to-all-start.4) | async-done | bytes 262176 | tf_op jit(solution)/shard_map/all_to_all | solution.py:68
  35.1 3.6 %all-to-all-start = ((bf16[128,32,128]{2,0,1:T(8,128)(2,1)}), bf16[128,32,128]{2,0,1:T(8,128)(2,1)S(1)}, u32[]{:S(2)}, u32[]{:S(2)}) async-start(bf16[128,32,128]{2,0,1:T(8,128)(2,1)} %copy.72), calls=%async_computation | async-start | bytes 2097152 | tf_op jit(solution)/shard_map/all_to_all | solution.py:65
  38.6 1.4 copy.75
  40.0 10.9 %all-to-all-done = bf16[128,32,128]{2,0,1:T(8,128)(2,1)S(1)} async-done(((bf16[128,32,128]{2,0,1:T(8,128)(2,1)}), bf16[128,32,128]{2,0,1:T(8,128)(2,1)S(1)}, u32[]{:S(2)}, u32[]{:S(2)}) %all-to-all-start) | async-done | bytes 1048608 | tf_op jit(solution)/shard_map/all_to_all | solution.py:65
  50.9 3.6 %all-to-all-start.3 = ((bf16[128,32,128]{2,0,1:T(8,128)(2,1)}), bf16[128,32,128]{2,0,1:T(8,128)(2,1)S(1)}, u32[]{:S(2)}, u32[]{:S(2)}) async-start(bf16[128,32,128]{2,0,1:T(8,128)(2,1)} %copy.75), calls=%async_computation.3 | async-start | bytes 2097152 | tf_op jit(solution)/shard_map/all_to_all | solution.py:66
  55.1 1.9 %collective-permute-start.1 = (bf16[512,1,128]{2,0,1:T(8,128)(2,1)S(1)}, bf16[512,1,128]{2,0,1:T(8,128)(2,1)S(1)}, u32[]{:S(2)}, u32[]{:S(2)}) collective-permute-start(bf16[512,1,128]{2,0,1:T(8,128)(2,1)S(1)} %bitcast.127), channel_id=1, source_target_pairs={{0,1},{1,2},{2,3},{3,4},{4,5},{5,6},{6,7},{7,8},{8,9},{9,10},{10,1... | collective-permute-start | bytes 393224 | tf_op jit(solution)/shard_map/ppermute | solution.py:15
  57.4 4.6 %collective-permute-start = (bf16[512,1,128]{2,0,1:T(8,128)(2,1)S(1)}, bf16[512,1,128]{2,0,1:T(8,128)(2,1)S(1)}, u32[]{:S(2)}, u32[]{:S(2)}) collective-permute-start(bf16[512,1,128]{2,0,1:T(8,128)(2,1)S(1)} %bitcast.126), channel_id=1, source_target_pairs={{0,1},{1,2},{2,3},{3,4},{4,5},{5,6},{6,7},{7,8},{8,9},{9,10},{10,1... | collective-permute-start | bytes 393224 | tf_op jit(solution)/shard_map/ppermute | solution.py:15
  62.0 7.3 %collective-permute-done.1 = bf16[512,1,128]{2,0,1:T(8,128)(2,1)S(1)} collective-permute-done((bf16[512,1,128]{2,0,1:T(8,128)(2,1)S(1)}, bf16[512,1,128]{2,0,1:T(8,128)(2,1)S(1)}, u32[]{:S(2)}, u32[]{:S(2)}) %collective-permute-start.1) | collective-permute-done | bytes 131104 | tf_op jit(solution)/shard_map/ppermute | solution.py:15
  69.4 4.5 %all-to-all-start.5 = ((f32[128,8,4]{0,2,1:T(4,128)}), f32[128,8,4]{0,2,1:T(4,128)S(1)}, u32[]{:S(2)}, u32[]{:S(2)}) async-start(f32[128,8,4]{0,2,1:T(4,128)} %bitcast.32), calls=%async_computation.5 | async-start | bytes 32768 | tf_op jit(solution)/shard_map/all_to_all | solution.py:73
  75.7 1.3 copy.76
  77.0 3.0 %all-to-all-done.5 = f32[128,8,4]{0,2,1:T(4,128)S(1)} async-done(((f32[128,8,4]{0,2,1:T(4,128)}), f32[128,8,4]{0,2,1:T(4,128)S(1)}, u32[]{:S(2)}, u32[]{:S(2)}) %all-to-all-start.5) | async-done | bytes 16416 | tf_op jit(solution)/shard_map/all_to_all | solution.py:73
  81.3 43.5 %while.19 = (s32[]{:T(128)}, bf16[1024,4,128]{2,0,1:T(8,128)(2,1)}, f32[1536,1,128]{2,0,1:T(8,128)S(1)}, f32[1536,1,128]{2,0,1:T(8,128)S(1)}, s32[]{:T(128)}, /*...) while((s32[]{:T(128)}, bf16[1024,4,128]{2,0,1:T(8,128)(2,1)}, ...), condition=%wide.region_4.5_spmd, body=%wide.region_3.4_spmd.sunk | while | flops 676857344 | bytes 13007369 | solution.py:146
  81.5 1.6 exponential_select_fusion.2
  84.1 1.4 fusion.54
  85.6 1.1 fusion.53
  86.9 1.6 exponential_select_fusion.2
  89.6 1.4 fusion.54
  91.0 1.1 fusion.53
  92.4 1.6 exponential_select_fusion.2
  95.0 1.4 fusion.54
  96.5 1.1 fusion.53
  97.8 1.6 exponential_select_fusion.2
  100.5 1.4 fusion.54
  103.3 1.6 exponential_select_fusion.2
  105.9 1.4 fusion.54
  108.7 1.6 exponential_select_fusion.2
  111.3 1.4 fusion.54
  114.1 1.6 exponential_select_fusion.2
  116.8 1.4 fusion.54
  119.6 1.6 exponential_select_fusion.2
  122.2 1.4 fusion.54
  124.8 1.9 %collective-permute-start.2 = (f32[512,1,128]{2,0,1:T(8,128)S(1)}, f32[512,1,128]{2,0,1:T(8,128)S(1)}, u32[]{:S(2)}, u32[]{:S(2)}) collective-permute-start(f32[512,1,128]{2,0,1:T(8,128)S(1)} %slice.47), channel_id=1, source_target_pairs={{1,0},{2,1},{3,2},{4,3},{5,4},{6,5},{7,6},{8,7},{9,8},{10,9},{11,1... | collective-permute-start | bytes 786440 | tf_op jit(solution)/shard_map/ppermute | solution.py:15
  126.8 3.3 %collective-permute-start.3 = (f32[512,1,128]{2,0,1:T(8,128)S(1)}, f32[512,1,128]{2,0,1:T(8,128)S(1)}, u32[]{:S(2)}, u32[]{:S(2)}) collective-permute-start(f32[512,1,128]{2,0,1:T(8,128)S(1)} %slice.50), channel_id=1, source_target_pairs={{1,0},{2,1},{3,2},{4,3},{5,4},{6,5},{7,6},{8,7},{9,8},{10,9},{11,1... | collective-permute-start | bytes 786440 | tf_op jit(solution)/shard_map/ppermute | solution.py:15
  130.1 6.1 %collective-permute-done.2 = f32[512,1,128]{2,0,1:T(8,128)S(1)} collective-permute-done((f32[512,1,128]{2,0,1:T(8,128)S(1)}, f32[512,1,128]{2,0,1:T(8,128)S(1)}, u32[]{:S(2)}, u32[]{:S(2)}) %collective-permute-start.2) | collective-permute-done | bytes 262176 | tf_op jit(solution)/shard_map/ppermute | solution.py:15
  138.4 3.4 %all-to-all-start.7 = ((bf16[8,2,8192]{2,1,0:T(2,128)(2,1)}), bf16[8,2,8192]{2,1,0:T(2,128)(2,1)S(1)}, u32[]{:S(2)}, u32[]{:S(2)}) async-start(bf16[8,2,8192]{2,1,0:T(2,128)(2,1)} %reshape.193), calls=%async_computation.7 | async-start | bytes 524288 | tf_op jit(solution)/shard_map/all_to_all | solution.py:158
  143.5 5.8 %all-to-all-done.7 = bf16[8,2,8192]{2,1,0:T(2,128)(2,1)S(1)} async-done(((bf16[8,2,8192]{2,1,0:T(2,128)(2,1)}), bf16[8,2,8192]{2,1,0:T(2,128)(2,1)S(1)}, u32[]{:S(2)}, u32[]{:S(2)}) %all-to-all-start.7) | async-done | bytes 262176 | tf_op jit(solution)/shard_map/all_to_all | solution.py:158
  149.2 3.4 %all-to-all-start.8 = ((bf16[8,2,8192]{2,1,0:T(2,128)(2,1)}), bf16[8,2,8192]{2,1,0:T(2,128)(2,1)S(1)}, u32[]{:S(2)}, u32[]{:S(2)}) async-start(bf16[8,2,8192]{2,1,0:T(2,128)(2,1)} %reshape.195), calls=%async_computation.8 | async-start | bytes 524288 | tf_op jit(solution)/shard_map/all_to_all | solution.py:161
  152.7 1.8 copy.78
  154.4 6.8 %all-to-all-done.8 = bf16[8,2,8192]{2,1,0:T(2,128)(2,1)S(1)} async-done(((bf16[8,2,8192]{2,1,0:T(2,128)(2,1)}), bf16[8,2,8192]{2,1,0:T(2,128)(2,1)S(1)}, u32[]{:S(2)}, u32[]{:S(2)}) %all-to-all-start.8) | async-done | bytes 262176 | tf_op jit(solution)/shard_map/all_to_all | solution.py:161
  161.2 3.6 %all-to-all-start.6 = ((bf16[1024,4,128]{2,1,0:T(4,128)(2,1)}), bf16[1024,4,128]{2,1,0:T(4,128)(2,1)S(1)}, u32[]{:S(2)}, u32[]{:S(2)}) async-start(bf16[1024,4,128]{2,1,0:T(4,128)(2,1)} %copy.78), calls=%async_computation.6 | async-start | bytes 2097152 | tf_op jit(solution)/shard_map/all_to_all | solution.py:156
  167.1 14.0 %all-to-all-done.6 = bf16[1024,4,128]{2,1,0:T(4,128)(2,1)S(1)} async-done(((bf16[1024,4,128]{2,1,0:T(4,128)(2,1)}), bf16[1024,4,128]{2,1,0:T(4,128)(2,1)S(1)}, u32[]{:S(2)}, u32[]{:S(2)}) %all-to-all-start.6) | async-done | bytes 1048608 | tf_op jit(solution)/shard_map/all_to_all | solution.py:156
  181.0 1.3 copy.79
  (116 shorter events, 28.8 us)
Async XLA Ops:
  0.6 27.2 %copy-start.2 = (bf16[128,32,128]{2,1,0:T(8,128)(2,1)S(1)}, bf16[128,32,128]{2,1,0:T(8,128)(2,1)}, u32[]{:S(2)}) copy-start(bf16[128,32,128]{2,1,0:T(8,128)(2,1)} %param.9) | copy-start | bytes 3145732
  0.6 11.7 %all-to-all-start.2 = ((f32[128,8,4]{0,2,1:T(4,128)}), f32[128,8,4]{0,2,1:T(4,128)S(1)}, u32[]{:S(2)}, u32[]{:S(2)}) async-start(f32[128,8,4]{0,2,1:T(4,128)} %bitcast.131), calls=%async_computation.2 | async-start | bytes 32768 | tf_op jit(solution)/shard_map/all_to_all | solution.py:72
  13.0 10.6 %all-to-all-start.1 = ((bf16[128,8,128]{2,0,1:T(8,128)(2,1)}), bf16[128,8,128]{2,0,1:T(8,128)(2,1)S(1)}, u32[]{:S(2)}, u32[]{:S(2)}) async-start(bf16[128,8,128]{2,0,1:T(8,128)(2,1)} %bitcast.14), calls=%async_computation.1 | async-start | bytes 524288 | tf_op jit(solution)/shard_map/all_to_all | solution.py:67
  24.4 10.6 %all-to-all-start.4 = ((bf16[128,8,128]{2,0,1:T(8,128)(2,1)}), bf16[128,8,128]{2,0,1:T(8,128)(2,1)S(1)}, u32[]{:S(2)}, u32[]{:S(2)}) async-start(bf16[128,8,128]{2,0,1:T(8,128)(2,1)} %bitcast.26), calls=%async_computation.4 | async-start | bytes 524288 | tf_op jit(solution)/shard_map/all_to_all | solution.py:68
  27.9 10.8 %copy-start.3 = (bf16[128,32,128]{2,1,0:T(8,128)(2,1)S(1)}, bf16[128,32,128]{2,1,0:T(8,128)(2,1)}, u32[]{:S(2)}) copy-start(bf16[128,32,128]{2,1,0:T(8,128)(2,1)} %param.12) | copy-start | bytes 3145732
  35.1 15.8 %all-to-all-start = ((bf16[128,32,128]{2,0,1:T(8,128)(2,1)}), bf16[128,32,128]{2,0,1:T(8,128)(2,1)S(1)}, u32[]{:S(2)}, u32[]{:S(2)}) async-start(bf16[128,32,128]{2,0,1:T(8,128)(2,1)} %copy.72), calls=%async_computation | async-start | bytes 2097152 | tf_op jit(solution)/shard_map/all_to_all | solution.py:65
  38.6 15.8 %copy-start.5 = (s32[256]{0:T(256)S(1)}, s32[256]{0:T(256)}, u32[]{:S(2)}) copy-start(s32[256]{0:T(256)} %param.15) | copy-start | bytes 3076
  50.9 18.4 %all-to-all-start.3 = ((bf16[128,32,128]{2,0,1:T(8,128)(2,1)}), bf16[128,32,128]{2,0,1:T(8,128)(2,1)S(1)}, u32[]{:S(2)}, u32[]{:S(2)}) async-start(bf16[128,32,128]{2,0,1:T(8,128)(2,1)} %copy.75), calls=%async_computation.3 | async-start | bytes 2097152 | tf_op jit(solution)/shard_map/all_to_all | solution.py:66
  55.1 14.2 %collective-permute-start.1 = (bf16[512,1,128]{2,0,1:T(8,128)(2,1)S(1)}, bf16[512,1,128]{2,0,1:T(8,128)(2,1)S(1)}, u32[]{:S(2)}, u32[]{:S(2)}) collective-permute-start(bf16[512,1,128]{2,0,1:T(8,128)(2,1)S(1)} %bitcast.127), channel_id=1, source_target_pairs={{0,1},{1,2},{2,3},{3,4},{4,5},{5,6},{6,7},{7,8},{8,9},{9,10},{10,1... | collective-permute-start | bytes 393224 | tf_op jit(solution)/shard_map/ppermute | solution.py:15
  57.4 16.4 %collective-permute-start = (bf16[512,1,128]{2,0,1:T(8,128)(2,1)S(1)}, bf16[512,1,128]{2,0,1:T(8,128)(2,1)S(1)}, u32[]{:S(2)}, u32[]{:S(2)}) collective-permute-start(bf16[512,1,128]{2,0,1:T(8,128)(2,1)S(1)} %bitcast.126), channel_id=1, source_target_pairs={{0,1},{1,2},{2,3},{3,4},{4,5},{5,6},{6,7},{7,8},{8,9},{9,10},{10,1... | collective-permute-start | bytes 393224 | tf_op jit(solution)/shard_map/ppermute | solution.py:15
  69.3 6.3 %copy-start = (bf16[128,32,128]{2,0,1:T(8,128)(2,1)}, bf16[128,32,128]{2,0,1:T(8,128)(2,1)S(1)}, u32[]{:S(2)}) copy-start(bf16[128,32,128]{2,0,1:T(8,128)(2,1)S(1)} %all-to-all-done.3) | copy-start | bytes 3145732
  69.4 10.7 %all-to-all-start.5 = ((f32[128,8,4]{0,2,1:T(4,128)}), f32[128,8,4]{0,2,1:T(4,128)S(1)}, u32[]{:S(2)}, u32[]{:S(2)}) async-start(f32[128,8,4]{0,2,1:T(4,128)} %bitcast.32), calls=%async_computation.5 | async-start | bytes 32768 | tf_op jit(solution)/shard_map/all_to_all | solution.py:73
  75.7 5.6 %copy-start.4 = (bf16[1536,1,128]{2,0,1:T(8,128)(2,1)S(1)}, bf16[1536,1,128]{2,0,1:T(8,128)(2,1)}, u32[]{:S(2)}) copy-start(bf16[1536,1,128]{2,0,1:T(8,128)(2,1)} %pad_maximum_fusion) | copy-start | bytes 1179652
  124.8 11.4 %collective-permute-start.2 = (f32[512,1,128]{2,0,1:T(8,128)S(1)}, f32[512,1,128]{2,0,1:T(8,128)S(1)}, u32[]{:S(2)}, u32[]{:S(2)}) collective-permute-start(f32[512,1,128]{2,0,1:T(8,128)S(1)} %slice.47), channel_id=1, source_target_pairs={{1,0},{2,1},{3,2},{4,3},{5,4},{6,5},{7,6},{8,7},{9,8},{10,9},{11,1... | collective-permute-start | bytes 786440 | tf_op jit(solution)/shard_map/ppermute | solution.py:15
  126.8 15.0 %collective-permute-start.3 = (f32[512,1,128]{2,0,1:T(8,128)S(1)}, f32[512,1,128]{2,0,1:T(8,128)S(1)}, u32[]{:S(2)}, u32[]{:S(2)}) collective-permute-start(f32[512,1,128]{2,0,1:T(8,128)S(1)} %slice.50), channel_id=1, source_target_pairs={{1,0},{2,1},{3,2},{4,3},{5,4},{6,5},{7,6},{8,7},{9,8},{10,9},{11,1... | collective-permute-start | bytes 786440 | tf_op jit(solution)/shard_map/ppermute | solution.py:15
  137.6 15.0 %copy-start.1 = (bf16[1024,4,128]{2,0,1:T(8,128)(2,1)S(1)}, bf16[1024,4,128]{2,0,1:T(8,128)(2,1)}, u32[]{:S(2)}) copy-start(bf16[1024,4,128]{2,0,1:T(8,128)(2,1)} %get-tuple-element.295) | copy-start | bytes 3145732
  138.4 10.8 %all-to-all-start.7 = ((bf16[8,2,8192]{2,1,0:T(2,128)(2,1)}), bf16[8,2,8192]{2,1,0:T(2,128)(2,1)S(1)}, u32[]{:S(2)}, u32[]{:S(2)}) async-start(bf16[8,2,8192]{2,1,0:T(2,128)(2,1)} %reshape.193), calls=%async_computation.7 | async-start | bytes 524288 | tf_op jit(solution)/shard_map/all_to_all | solution.py:158
  149.2 12.0 %all-to-all-start.8 = ((bf16[8,2,8192]{2,1,0:T(2,128)(2,1)}), bf16[8,2,8192]{2,1,0:T(2,128)(2,1)S(1)}, u32[]{:S(2)}, u32[]{:S(2)}) async-start(bf16[8,2,8192]{2,1,0:T(2,128)(2,1)} %reshape.195), calls=%async_computation.8 | async-start | bytes 524288 | tf_op jit(solution)/shard_map/all_to_all | solution.py:161
  161.2 19.8 %all-to-all-start.6 = ((bf16[1024,4,128]{2,1,0:T(4,128)(2,1)}), bf16[1024,4,128]{2,1,0:T(4,128)(2,1)S(1)}, u32[]{:S(2)}, u32[]{:S(2)}) async-start(bf16[1024,4,128]{2,1,0:T(4,128)(2,1)} %copy.78), calls=%async_computation.6 | async-start | bytes 2097152 | tf_op jit(solution)/shard_map/all_to_all | solution.py:156
where the time goes:
time: 184 us; the launch traced here: 182 us
  waiting for transfers between devices  71.2 us (39%)
  starting transfers between devices  46 us (25%)
  matrix products  41.4 us (22%)
  local copies, waits for them, and re-layouts  19.1 us (10%)
  other arithmetic  3.47 us (2%)
    dot_general x16, matrix products, across_cols(): lax.dot_general(left, right, (((1,), (1,)), ((), ())), preferred_element_...  16.7 us
    dot_general x16, matrix products, across_rows(): lax.dot_general(left, right, (((0,), (0,)), ((), ())), preferred_element_...  15.8 us
    all_to_all x1, waiting for transfers between devices, shards(): lax.all_to_all(query_total, 'head', split_axis=0, concat_axis=1, tiled=True)  14 us
    ppermute x4, waiting for transfers between devices, shifted(): return lax.ppermute(x, axis, pairs)  13.4 us
    ppermute x4, starting transfers between devices, shifted(): return lax.ppermute(x, axis, pairs)  11.7 us
    all_to_all x1, waiting for transfers between devices, shards(): lax.all_to_all(query_states, 'head', split_axis=1, concat_axis=0, tiled=T...  10.9 us
    dot_general x8, matrix products, tile_terms(): jnp.dot(score_grad, key_cols, preferred_element_type=jnp.float32)  8.89 us
    unnamed x24, local copies, waits for them, and re-layouts  8.3 us
  transfers between devices with their start and end apart: 13, of which 10 were waited for; matrix products, arithmetic and copies ran while one was open for 9% of the time, Pallas kernels for 0%

commit v1 on v0

v1 whole, which is shorter than its diff:
```python
import functools
import math

import jax
import jax.numpy as jnp
from jax import lax
from jax.experimental import pallas as pl
from jax.experimental.pallas import tpu as pltpu
from jax.sharding import PartitionSpec as P

KV_HEADS = 4
HEAD_DIM = 128
MOST = 512
LOG2E = 1.4426950408889634
VMEM_LIMIT = 40 * 1024 * 1024


def doc_starts(doc_lengths, positions):
    doc_ends = jnp.cumsum(doc_lengths)
    before = jnp.where(doc_ends[None, :] <= positions[:, None], doc_lengths[None, :], 0)
    return jnp.sum(before, axis=1)


def chunk_shift(x, by):
    heads, ctxs = lax.axis_size("head"), lax.axis_size("ctx")
    count = heads * ctxs
    place = lambda c: (c % heads) * ctxs + c // heads
    pairs = [(place(c), place(c + by)) for c in range(count) if 0 <= c + by < count]
    return lax.ppermute(x, ("head", "ctx"), pairs)


def contract(left, right, dims):
    return lax.dot_general(
        left, right, ((dims[:1], dims[1:]), ((), ())), preferred_element_type=jnp.float32
    )


def tile_kernel(
    distance,
    first,
    last,
    softmax_scale,
    start_ref,
    norm_ref,
    delta_ref,
    query_ref,
    grad_ref,
    kv_ref,
    *rest,
):
    if first:
        query_total_ref, kv_part_ref = rest
    else:
        query_in_ref, query_total_ref, kv_part_ref = rest
    rows = kv_ref.shape[2]
    cols = query_ref.shape[1]
    step = 2 * rows
    keys = kv_ref[0, 0]
    values = kv_ref[1, 0]
    key_part = jnp.zeros((rows, HEAD_DIM), jnp.float32)
    value_part = jnp.zeros((rows, HEAD_DIM), jnp.float32)
    key_pos = lax.broadcasted_iota(jnp.int32, (rows, step), 0) - distance * rows
    if distance == 0:
        query_pos = lax.broadcasted_iota(jnp.int32, (rows, step), 1) & (rows - 1)
        causal = key_pos <= query_pos
    for at in range(0, cols, step):
        span = pl.ds(at, step)
        query_rows = query_ref[0, span, :]
        grad_rows = grad_ref[0, span, :]
        scores = contract(keys, query_rows, (1, 1))
        prob_grad = contract(values, grad_rows, (1, 1))
        prob = jnp.exp2(scores * (softmax_scale * LOG2E) - norm_ref[0, :, span] * LOG2E)
        allowed = key_pos >= start_ref[:, span]
        if distance == 0:
            allowed = allowed & causal
        prob = jnp.where(allowed, prob, 0.0)
        score_grad = (prob * (prob_grad - delta_ref[0, :, span])).astype(jnp.bfloat16)
        value_part += contract(prob.astype(jnp.bfloat16), grad_rows, (1, 0))
        key_part += contract(score_grad, query_rows, (1, 0))
        query_part = contract(keys, score_grad, (0, 0))
        if not first:
            query_part += query_in_ref[0, :, span]
        if last:
            for head in range(at // rows, (at + step) // rows):
                part = query_part[:, head * rows - at : (head + 1) * rows - at]
                query_total_ref[0, head] = (part.T * softmax_scale).astype(jnp.bfloat16)
        else:
            query_total_ref[0, :, span] = query_part
    kv_part_ref[0, 0] = (key_part * softmax_scale).astype(kv_part_ref.dtype)
    kv_part_ref[1, 0] = value_part.astype(kv_part_ref.dtype)


def tile_call(distance, first, last, starts, norms, deltas, queries, grads, kv, query_total=None):
    groups, cols, dim = queries.shape
    rows = kv.shape[2]
    softmax_scale = 1.0 / math.sqrt(HEAD_DIM)
    row_spec = pl.BlockSpec((1, 1, cols), lambda g: (g, 0, 0))
    wide_spec = pl.BlockSpec((1, cols, dim), lambda g: (g, 0, 0))
    kv_spec = pl.BlockSpec((2, 1, rows, dim), lambda g: (0, g, 0, 0))
    total_spec = pl.BlockSpec((1, dim, cols), lambda g: (g, 0, 0))
    in_specs = [
        pl.BlockSpec((1, cols), lambda g: (0, 0)),
        row_spec,
        row_spec,
        wide_spec,
        wide_spec,
        kv_spec,
    ]
    args = [starts, norms, deltas, queries, grads, kv]
    if not first:
        in_specs.append(total_spec)
        args.append(query_total)
    if last:
        heads = cols // rows
        query_shape = jax.ShapeDtypeStruct((groups, heads, rows, dim), jnp.bfloat16)
        query_spec = pl.BlockSpec((1, heads, rows, dim), lambda g: (g, 0, 0, 0))
    else:
        query_shape = jax.ShapeDtypeStruct((groups, dim, cols), jnp.float32)
        query_spec = total_spec
    kv_shape = jax.ShapeDtypeStruct(kv.shape, jnp.float32 if distance == 0 else jnp.bfloat16)
    return pl.pallas_call(
        functools.partial(tile_kernel, distance, first, last, softmax_scale),
        grid=(groups,),
        in_specs=in_specs,
        out_specs=(query_spec, kv_spec),
        out_shape=(query_shape, kv_shape),
        compiler_params=pltpu.CompilerParams(vmem_limit_bytes=VMEM_LIMIT),
        cost_estimate=pl.CostEstimate(
            flops=10 * groups * cols * rows * dim,
            bytes_accessed=6 * groups * cols * dim,
            transcendentals=groups * cols * rows,
        ),
        name=f"tiles_{distance}",
    )(*args)


def shards(query_states, key_states, value_states, out_grad, log_norm, row_delta, doc_lengths):
    rows, heads, dim = query_states.shape
    group = heads // KV_HEADS
    reach = MOST // rows
    chunk = lax.axis_index("ctx") * lax.axis_size("head") + lax.axis_index("head")
    first_pos = chunk * rows

    kv = jnp.transpose(jnp.stack([key_states, value_states]), (0, 2, 1, 3))
    behind = {distance: chunk_shift(kv, distance) for distance in range(reach, 0, -1)}

    by_head = lambda x: jnp.transpose(x, (1, 0, 2)).reshape(KV_HEADS, group * rows, dim)
    queries, grads = by_head(query_states), by_head(out_grad)
    norms = log_norm.T.reshape(KV_HEADS, 1, group * rows)
    deltas = row_delta.T.reshape(KV_HEADS, 1, group * rows)
    positions = first_pos + jnp.arange(rows, dtype=jnp.int32)
    starts = doc_starts(doc_lengths, positions) - first_pos
    starts = jnp.tile(starts, group).reshape(1, group * rows)

    query_total, kv_own = tile_call(0, True, False, starts, norms, deltas, queries, grads, kv)
    returned = []
    for distance in range(reach, 0, -1):
        query_total, kv_part = tile_call(
            distance,
            False,
            distance == 1,
            starts,
            norms,
            deltas,
            queries,
            grads,
            behind[distance],
            query_total,
        )
        returned.append(chunk_shift(kv_part, -distance))
    for part in returned:
        kv_own = kv_own + part.astype(jnp.float32)
    kv_grad = jnp.transpose(kv_own.astype(jnp.bfloat16), (0, 2, 1, 3))
    query_grad = jnp.transpose(query_total.reshape(heads, rows, dim), (1, 0, 2))
    return (query_grad, kv_grad[0], kv_grad[1])


def solution(mesh):
    spec3 = P(("ctx", "head"), None, None)
    spec2 = P(("ctx", "head"), None)
    return jax.shard_map(
        shards,
        mesh=mesh,
        in_specs=(spec3, spec3, spec3, spec3, spec2, spec2, P()),
        out_specs=(spec3, spec3, spec3),
        check_vma=False,
    )
```

time: 184 us -> 77.2 us (0.42)
  the two profiles are of different devices: /device:TPU:256 before, /device:TPU:253 now
where the time goes in v1:
time: 77.2 us; the launch traced here: 76.9 us
  starting transfers between devices  28 us (36%)
  Pallas kernels  19.9 us (26%)
  waiting for transfers between devices  19.4 us (25%)
  local copies, waits for them, and re-layouts  6.54 us (8%)
  other arithmetic  2.15 us (3%)
  between operations  0.88 us (1%)
    ppermute x8, starting transfers between devices, chunk_shift(): return lax.ppermute(x, ('head', 'ctx'), pairs)  28 us
    pallas_call x5, Pallas kernels, tile_call(): pl.pallas_call(functools.partial(tile_kernel, distance, first, last, soft...  19.9 us
    ppermute x8, waiting for transfers between devices, chunk_shift(): return lax.ppermute(x, ('head', 'ctx'), pairs)  19.4 us
    transpose x2, local copies, waits for them, and re-layouts, shards(): jnp.transpose(x, (1, 0, 2)).reshape(KV_HEADS, group * rows, dim)  2.05 us
    reshape x1, local copies, waits for them, and re-layouts, shards(): query_grad = jnp.transpose(query_total.reshape(heads, rows, dim), (1, 0, 2))  1.65 us
  transfers between devices with their start and end apart: 8, of which 3 were waited for; matrix products, arithmetic and copies ran while one was open for 8% of the time, Pallas kernels for 20%

profile of v1, /device:TPU:253, one launch (start us, length us, event | category | flops | bytes accessed | tf_op | source)
XLA Modules:
  0.0 76.9 jit_solution(1912424155651203095)
XLA Ops:
  0.6 0.0 copy-start.2
  0.6 1.1 %copy_bitcast_fusion.1 = (bf16[1,128,4,128]{3,1,2,0:T(8,128)(2,1)S(1)}, bf16[1,128,4,128]{3,1,2,0:T(8,128)(2,1)S(1)}) fusion(bf16[128,4,128]{2,1,0:T(4,128)(2,1)} %param.9, bf16[128,4,128]{2,1,0:T(4,128)(2,1)} %param.8), kind=kLoop, calls=%fused_computation.6 | loop fusion | bytes 524288 | tf_op jit(solution)/shard_map/stack | solution.py:144
  1.8 5.9 %collective-permute-start.3 = (bf16[2,4,128,128]{3,2,1,0:T(8,128)(2,1)S(1)}, bf16[2,4,128,128]{3,2,1,0:T(8,128)(2,1)S(1)}, u32[]{:S(2)}, u32[]{:S(2)}) collective-permute-start(bf16[2,4,128,128]{3,2,1,0:T(8,128)(2,1)S(1)} %maximum_bitcast_fusion.kv_ref), channel_id=1, source_target_pairs={{0,256},{64,320},{128,384},{192,448},{256,1},{320,65},{384,129},{4... | collective-permute-start | bytes 786440 | tf_op jit(solution)/shard_map/ppermute | solution.py:29
  7.7 3.9 %collective-permute-start.2 = (bf16[2,4,128,128]{3,2,1,0:T(8,128)(2,1)S(1)}, bf16[2,4,128,128]{3,2,1,0:T(8,128)(2,1)S(1)}, u32[]{:S(2)}, u32[]{:S(2)}) collective-permute-start(bf16[2,4,128,128]{3,2,1,0:T(8,128)(2,1)S(1)} %maximum_bitcast_fusion.kv_ref), channel_id=1, source_target_pairs={{0,192},{64,256},{128,320},{192,384},{256,448},{320,1},{384,65},{4... | collective-permute-start | bytes 786440 | tf_op jit(solution)/shard_map/ppermute | solution.py:29
  11.6 2.8 %collective-permute-start.1 = (bf16[2,4,128,128]{3,2,1,0:T(8,128)(2,1)S(1)}, bf16[2,4,128,128]{3,2,1,0:T(8,128)(2,1)S(1)}, u32[]{:S(2)}, u32[]{:S(2)}) collective-permute-start(bf16[2,4,128,128]{3,2,1,0:T(8,128)(2,1)S(1)} %maximum_bitcast_fusion.kv_ref), channel_id=1, source_target_pairs={{0,128},{64,192},{128,256},{192,320},{256,384},{320,448},{384,1},{... | collective-permute-start | bytes 786440 | tf_op jit(solution)/shard_map/ppermute | solution.py:29
  14.5 4.4 %collective-permute-start = (bf16[2,4,128,128]{3,2,1,0:T(8,128)(2,1)S(1)}, bf16[2,4,128,128]{3,2,1,0:T(8,128)(2,1)S(1)}, u32[]{:S(2)}, u32[]{:S(2)}) collective-permute-start(bf16[2,4,128,128]{3,2,1,0:T(8,128)(2,1)S(1)} %maximum_bitcast_fusion.kv_ref), channel_id=1, source_target_pairs={{0,64},{64,128},{128,192},{192,256},{256,320},{320,384},{384,448},... | collective-permute-start | bytes 786440 | tf_op jit(solution)/shard_map/ppermute | solution.py:29
  18.9 1.0 %reduce-window.9 = s32[2,128]{1,0:T(2,128)S(1)} reduce-window(s32[2,128]{1,0:T(2,128)} %bitcast.59, s32[]{:T(128)} %constant.6.clone.1), window={size=1x128 pad=0_0x127_0}, to_apply=%region_0.0 | reduce-window | flops 32512 | bytes 2052 | tf_op jit(solution)/shard_map/reduce-window
  19.9 0.1 slice.13
  20.0 0.1 slice_reduce_fusion
  20.1 0.1 add_bitcast_fusion
  20.2 0.8 %select_reduce_fusion = s32[128]{0:T(128)S(1)} fusion(s32[256]{0:T(256)} %param.13, s32[256]{0:T(256)S(1)} %add_bitcast_fusion, s32[128]{0:T(128)S(1)} %iota_add_fusion), kind=kLoop, calls=%fused_computation.8 | loop fusion | flops 98176 | bytes 3072 | tf_op jit(solution)/shard_map/reduce_sum | solution.py:21
  21.0 0.0 copy-start
  21.0 0.0 copy-start.1
  21.1 1.6 %copy.24 = bf16[32,128,128]{2,1,0:T(8,128)(2,1)S(1)} copy(bf16[32,128,128]{2,0,1:T(8,128)(2,1)} %bitcast.56) | data formatting | bytes 2097152 | tf_op jit(solution)/shard_map/transpose | solution.py:147
  22.7 0.0 copy-done.2
  22.7 0.4 copy.25
  23.1 0.0 copy-done
  23.2 0.0 copy-done.1
  23.2 4.0 %tiles_0.1 = (f32[4,128,1024]{2,1,0:T(8,128)S(1)}, f32[2,4,128,128]{3,2,1,0:T(8,128)S(1)}) custom-call(s32[1,1024]{1,0:T(1,128)S(1)} %bitcast.51, f32[4,1,1024]{2,1,0:T(1,128)S(1)} %bitcast.41, f32[4,1,1024]{2,1,0:T(1,128)S(1)} %bitcast.46, bf16[4,1024,128]{2,1,0:T(8,128)(2,1)S(1)} %bitcast.30, bf16[4,1024,128]{2,1,0:T(8,128)(2,1)S(1)} %bitcast.35, ...), custom_call_target="tpu_custom_call" | custom-call | flops 671088640 | bytes 3145728 | tf_op jit(solution)/shard_map/tiles_0/pallas_call | solution.py:121
  27.2 0.0 collective-permute-done.3.kv_ref
  27.2 3.9 %tiles_4.1 = (f32[4,128,1024]{2,1,0:T(8,128)S(1)}, bf16[2,4,128,128]{3,2,1,0:T(8,128)(2,1)S(1)}) custom-call(s32[1,1024]{1,0:T(1,128)S(1)} %bitcast.52, f32[4,1,1024]{2,1,0:T(1,128)S(1)} %bitcast.42, f32[4,1,1024]{2,1,0:T(1,128)S(1)} %bitcast.47, bf16[4,1024,128]{2,1,0:T(8,128)(2,1)S(1)} %bitcast.31, bf16[4,1024,128]{2,1,0:T(8,128)(2,1)S(1)} %bitcast.36, ...), custom_call_target="tpu_custom_call" | custom-call | flops 671088640 | bytes 3145728 | tf_op jit(solution)/shard_map/tiles_4/pallas_call | solution.py:121
  31.1 0.0 collective-permute-done.2.kv_ref
  31.1 3.9 %tiles_3.1 = (f32[4,128,1024]{2,1,0:T(8,128)S(1)}, bf16[2,4,128,128]{3,2,1,0:T(8,128)(2,1)S(1)}) custom-call(s32[1,1024]{1,0:T(1,128)S(1)} %bitcast.53, f32[4,1,1024]{2,1,0:T(1,128)S(1)} %bitcast.43, f32[4,1,1024]{2,1,0:T(1,128)S(1)} %bitcast.48, bf16[4,1024,128]{2,1,0:T(8,128)(2,1)S(1)} %bitcast.32, bf16[4,1024,128]{2,1,0:T(8,128)(2,1)S(1)} %bitcast.37, ...), custom_call_target="tpu_custom_call" | custom-call | flops 671088640 | bytes 3145728 | tf_op jit(solution)/shard_map/tiles_3/pallas_call | solution.py:121
  35.0 0.0 collective-permute-done.1.kv_ref
  35.0 3.9 %tiles_2.1 = (f32[4,128,1024]{2,1,0:T(8,128)S(1)}, bf16[2,4,128,128]{3,2,1,0:T(8,128)(2,1)S(1)}) custom-call(s32[1,1024]{1,0:T(1,128)S(1)} %bitcast.54, f32[4,1,1024]{2,1,0:T(1,128)S(1)} %bitcast.44, f32[4,1,1024]{2,1,0:T(1,128)S(1)} %bitcast.49, bf16[4,1024,128]{2,1,0:T(8,128)(2,1)S(1)} %bitcast.33, bf16[4,1024,128]{2,1,0:T(8,128)(2,1)S(1)} %bitcast.38, ...), custom_call_target="tpu_custom_call" | custom-call | flops 671088640 | bytes 3145728 | tf_op jit(solution)/shard_map/tiles_2/pallas_call | solution.py:121
  38.9 0.0 collective-permute-done.kv_ref
  38.9 4.2 %tiles_1.1 = (bf16[4,8,128,128]{3,2,1,0:T(8,128)(2,1)S(1)}, bf16[2,4,128,128]{3,2,1,0:T(8,128)(2,1)S(1)}) custom-call(s32[1,1024]{1,0:T(1,128)S(1)} %bitcast.55, f32[4,1,1024]{2,1,0:T(1,128)S(1)} %bitcast.45, f32[4,1,1024]{2,1,0:T(1,128)S(1)} %bitcast.50, bf16[4,1024,128]{2,1,0:T(8,128)(2,1)S(1)} %bitcast.34, bf16[4,1024,128]{2,1,0:T(8,128)(2,1)S(1)} %bitcast.39, ...), custom_call_target="tpu_custom_call" | custom-call | flops 671088640 | bytes 3145728 | tf_op jit(solution)/shard_map/tiles_1/pallas_call | solution.py:121
  43.1 1.9 %collective-permute-start.7 = (bf16[2,4,128,128]{3,2,1,0:T(8,128)(2,1)S(1)}, bf16[2,4,128,128]{3,2,1,0:T(8,128)(2,1)S(1)}, u32[]{:S(2)}, u32[]{:S(2)}) collective-permute-start(bf16[2,4,128,128]{3,2,1,0:T(8,128)(2,1)S(1)} %get-tuple-element.22), channel_id=1, source_target_pairs={{64,0},{128,64},{192,128},{256,192},{320,256},{384,320},{448,384},... | collective-permute-start | bytes 786440 | tf_op jit(solution)/shard_map/ppermute | solution.py:29
  45.1 2.8 %collective-permute-start.6 = (bf16[2,4,128,128]{3,2,1,0:T(8,128)(2,1)S(1)}, bf16[2,4,128,128]{3,2,1,0:T(8,128)(2,1)S(1)}, u32[]{:S(2)}, u32[]{:S(2)}) collective-permute-start(bf16[2,4,128,128]{3,2,1,0:T(8,128)(2,1)S(1)} %get-tuple-element.21), channel_id=1, source_target_pairs={{128,0},{192,64},{256,128},{320,192},{384,256},{448,320},{1,384},{... | collective-permute-start | bytes 786440 | tf_op jit(solution)/shard_map/ppermute | solution.py:29
  47.9 3.3 %collective-permute-start.5 = (bf16[2,4,128,128]{3,2,1,0:T(8,128)(2,1)S(1)}, bf16[2,4,128,128]{3,2,1,0:T(8,128)(2,1)S(1)}, u32[]{:S(2)}, u32[]{:S(2)}) collective-permute-start(bf16[2,4,128,128]{3,2,1,0:T(8,128)(2,1)S(1)} %get-tuple-element.20), channel_id=1, source_target_pairs={{192,0},{256,64},{320,128},{384,192},{448,256},{1,320},{65,384},{1... | collective-permute-start | bytes 786440 | tf_op jit(solution)/shard_map/ppermute | solution.py:29
  51.2 3.0 %collective-permute-start.4 = (bf16[2,4,128,128]{3,2,1,0:T(8,128)(2,1)S(1)}, bf16[2,4,128,128]{3,2,1,0:T(8,128)(2,1)S(1)}, u32[]{:S(2)}, u32[]{:S(2)}) collective-permute-start(bf16[2,4,128,128]{3,2,1,0:T(8,128)(2,1)S(1)} %get-tuple-element.19), channel_id=1, source_target_pairs={{256,0},{320,64},{384,128},{448,192},{1,256},{65,320},{129,384},{1... | collective-permute-start | bytes 786440 | tf_op jit(solution)/shard_map/ppermute | solution.py:29
  54.1 1.6 %copy.34 = bf16[32,128,128]{2,0,1:T(8,128)(2,1)} copy(bf16[32,128,128]{2,1,0:T(8,128)(2,1)S(1)} %bitcast.40) | data formatting | bytes 2097152 | tf_op jit(solution)/shard_map/reshape | solution.py:174
  55.8 0.0 collective-permute-done.7
  55.8 7.6 %collective-permute-done.6 = bf16[2,4,128,128]{3,2,1,0:T(8,128)(2,1)S(1)} collective-permute-done((bf16[2,4,128,128]{3,2,1,0:T(8,128)(2,1)S(1)}, bf16[2,4,128,128]{3,2,1,0:T(8,128)(2,1)S(1)}, u32[]{:S(2)}, u32[]{:S(2)}) %collective-permute-start.6) | collective-permute-done | bytes 262176 | tf_op jit(solution)/shard_map/ppermute | solution.py:29
  63.4 1.8 %collective-permute-done.5 = bf16[2,4,128,128]{3,2,1,0:T(8,128)(2,1)S(1)} collective-permute-done((bf16[2,4,128,128]{3,2,1,0:T(8,128)(2,1)S(1)}, bf16[2,4,128,128]{3,2,1,0:T(8,128)(2,1)S(1)}, u32[]{:S(2)}, u32[]{:S(2)}) %collective-permute-start.5) | collective-permute-done | bytes 262176 | tf_op jit(solution)/shard_map/ppermute | solution.py:29
  65.3 9.9 %collective-permute-done.4 = bf16[2,4,128,128]{3,2,1,0:T(8,128)(2,1)S(1)} collective-permute-done((bf16[2,4,128,128]{3,2,1,0:T(8,128)(2,1)S(1)}, bf16[2,4,128,128]{3,2,1,0:T(8,128)(2,1)S(1)}, u32[]{:S(2)}, u32[]{:S(2)}) %collective-permute-start.4) | collective-permute-done | bytes 262176 | tf_op jit(solution)/shard_map/ppermute | solution.py:29
  75.1 0.2 fusion
  75.3 0.8 copy.30
  76.1 0.8 copy.29
  (6 shorter events, 0.1 us)
Async XLA Ops:
  0.6 22.1 %copy-start.2 = (bf16[128,32,128]{2,1,0:T(8,128)(2,1)S(1)}, bf16[128,32,128]{2,1,0:T(8,128)(2,1)}, u32[]{:S(2)}) copy-start(bf16[128,32,128]{2,1,0:T(8,128)(2,1)} %param.10) | copy-start | bytes 3145732
  1.8 25.4 %collective-permute-start.3 = (bf16[2,4,128,128]{3,2,1,0:T(8,128)(2,1)S(1)}, bf16[2,4,128,128]{3,2,1,0:T(8,128)(2,1)S(1)}, u32[]{:S(2)}, u32[]{:S(2)}) collective-permute-start(bf16[2,4,128,128]{3,2,1,0:T(8,128)(2,1)S(1)} %maximum_bitcast_fusion.kv_ref), channel_id=1, source_target_pairs={{0,256},{64,320},{128,384},{192,448},{256,1},{320,65},{384,129},{4... | collective-permute-start | bytes 786440 | tf_op jit(solution)/shard_map/ppermute | solution.py:29
  7.7 23.4 %collective-permute-start.2 = (bf16[2,4,128,128]{3,2,1,0:T(8,128)(2,1)S(1)}, bf16[2,4,128,128]{3,2,1,0:T(8,128)(2,1)S(1)}, u32[]{:S(2)}, u32[]{:S(2)}) collective-permute-start(bf16[2,4,128,128]{3,2,1,0:T(8,128)(2,1)S(1)} %maximum_bitcast_fusion.kv_ref), channel_id=1, source_target_pairs={{0,192},{64,256},{128,320},{192,384},{256,448},{320,1},{384,65},{4... | collective-permute-start | bytes 786440 | tf_op jit(solution)/shard_map/ppermute | solution.py:29
  11.6 23.4 %collective-permute-start.1 = (bf16[2,4,128,128]{3,2,1,0:T(8,128)(2,1)S(1)}, bf16[2,4,128,128]{3,2,1,0:T(8,128)(2,1)S(1)}, u32[]{:S(2)}, u32[]{:S(2)}) collective-permute-start(bf16[2,4,128,128]{3,2,1,0:T(8,128)(2,1)S(1)} %maximum_bitcast_fusion.kv_ref), channel_id=1, source_target_pairs={{0,128},{64,192},{128,256},{192,320},{256,384},{320,448},{384,1},{... | collective-permute-start | bytes 786440 | tf_op jit(solution)/shard_map/ppermute | solution.py:29
  14.5 24.5 %collective-permute-start = (bf16[2,4,128,128]{3,2,1,0:T(8,128)(2,1)S(1)}, bf16[2,4,128,128]{3,2,1,0:T(8,128)(2,1)S(1)}, u32[]{:S(2)}, u32[]{:S(2)}) collective-permute-start(bf16[2,4,128,128]{3,2,1,0:T(8,128)(2,1)S(1)} %maximum_bitcast_fusion.kv_ref), channel_id=1, source_target_pairs={{0,64},{64,128},{128,192},{192,256},{256,320},{320,384},{384,448},... | collective-permute-start | bytes 786440 | tf_op jit(solution)/shard_map/ppermute | solution.py:29
  21.0 2.1 %copy-start = (f32[128,32]{0,1:T(8,128)S(1)}, f32[128,32]{0,1:T(8,128)}, u32[]{:S(2)}) copy-start(f32[128,32]{0,1:T(8,128)} %param.11) | copy-start | bytes 49156
  21.0 2.1 %copy-start.1 = (f32[128,32]{0,1:T(8,128)S(1)}, f32[128,32]{0,1:T(8,128)}, u32[]{:S(2)}) copy-start(f32[128,32]{0,1:T(8,128)} %param.12) | copy-start | bytes 49156
  43.1 12.7 %collective-permute-start.7 = (bf16[2,4,128,128]{3,2,1,0:T(8,128)(2,1)S(1)}, bf16[2,4,128,128]{3,2,1,0:T(8,128)(2,1)S(1)}, u32[]{:S(2)}, u32[]{:S(2)}) collective-permute-start(bf16[2,4,128,128]{3,2,1,0:T(8,128)(2,1)S(1)} %get-tuple-element.22), channel_id=1, source_target_pairs={{64,0},{128,64},{192,128},{256,192},{320,256},{384,320},{448,384},... | collective-permute-start | bytes 786440 | tf_op jit(solution)/shard_map/ppermute | solution.py:29
  45.1 18.4 %collective-permute-start.6 = (bf16[2,4,128,128]{3,2,1,0:T(8,128)(2,1)S(1)}, bf16[2,4,128,128]{3,2,1,0:T(8,128)(2,1)S(1)}, u32[]{:S(2)}, u32[]{:S(2)}) collective-permute-start(bf16[2,4,128,128]{3,2,1,0:T(8,128)(2,1)S(1)} %get-tuple-element.21), channel_id=1, source_target_pairs={{128,0},{192,64},{256,128},{320,192},{384,256},{448,320},{1,384},{... | collective-permute-start | bytes 786440 | tf_op jit(solution)/shard_map/ppermute | solution.py:29
  47.9 17.4 %collective-permute-start.5 = (bf16[2,4,128,128]{3,2,1,0:T(8,128)(2,1)S(1)}, bf16[2,4,128,128]{3,2,1,0:T(8,128)(2,1)S(1)}, u32[]{:S(2)}, u32[]{:S(2)}) collective-permute-start(bf16[2,4,128,128]{3,2,1,0:T(8,128)(2,1)S(1)} %get-tuple-element.20), channel_id=1, source_target_pairs={{192,0},{256,64},{320,128},{384,192},{448,256},{1,320},{65,384},{1... | collective-permute-start | bytes 786440 | tf_op jit(solution)/shard_map/ppermute | solution.py:29
  51.2 24.0 %collective-permute-start.4 = (bf16[2,4,128,128]{3,2,1,0:T(8,128)(2,1)S(1)}, bf16[2,4,128,128]{3,2,1,0:T(8,128)(2,1)S(1)}, u32[]{:S(2)}, u32[]{:S(2)}) collective-permute-start(bf16[2,4,128,128]{3,2,1,0:T(8,128)(2,1)S(1)} %get-tuple-element.19), channel_id=1, source_target_pairs={{256,0},{320,64},{384,128},{448,192},{1,256},{65,320},{129,384},{1... | collective-permute-start | bytes 786440 | tf_op jit(solution)/shard_map/ppermute | solution.py:29

commit v2 on v1

v2 whole, which is shorter than its diff:
```python
import functools
import math

import jax
import jax.numpy as jnp
from jax import lax
from jax.experimental import pallas as pl
from jax.experimental.pallas import tpu as pltpu
from jax.sharding import PartitionSpec as P

KV_HEADS = 4
HEAD_DIM = 128
MOST = 512
LOG2E = 1.4426950408889634
VMEM_LIMIT = 40 * 1024 * 1024
WEIGHT = 1
SUM_FLOPS = 5_000_000_000


def doc_starts(doc_lengths, positions):
    doc_ends = jnp.cumsum(doc_lengths)
    before = jnp.where(doc_ends[None, :] <= positions[:, None], doc_lengths[None, :], 0)
    return jnp.sum(before, axis=1)


def chunk_shift(x, by):
    heads, ctxs = lax.axis_size("head"), lax.axis_size("ctx")
    count = heads * ctxs
    place = lambda c: (c % heads) * ctxs + c // heads
    pairs = [(place(c), place(c + by)) for c in range(count) if 0 <= c + by < count]
    return lax.ppermute(x, ("head", "ctx"), pairs)


def contract(left, right, dims):
    return lax.dot_general(
        left, right, ((dims[:1], dims[1:]), ((), ())), preferred_element_type=jnp.float32
    )


def tile_kernel(
    distance,
    softmax_scale,
    start_ref,
    norm_ref,
    delta_ref,
    query_ref,
    grad_ref,
    kv_ref,
    *rest,
):
    query_in_ref = rest[0] if len(rest) == 3 else None
    query_total_ref, kv_part_ref = rest[-2:]
    groups, cols, _ = query_ref.shape
    rows = kv_ref.shape[2]
    key_pos = lax.broadcasted_iota(jnp.int32, (rows, cols), 0) - distance * rows
    allowed = key_pos >= start_ref[...]
    if distance == 0:
        query_pos = lax.broadcasted_iota(jnp.int32, (rows, cols), 1) & (rows - 1)
        allowed = allowed & (key_pos <= query_pos)
    for group in range(groups):
        keys = kv_ref[0, group]
        values = kv_ref[1, group]
        query_rows = query_ref[group]
        grad_rows = grad_ref[group]
        scores = contract(keys, query_rows, (1, 1))
        prob_grad = contract(values, grad_rows, (1, 1))
        prob = jnp.exp2(scores * (softmax_scale * LOG2E) - norm_ref[group])
        prob = jnp.where(allowed, prob, 0.0)
        score_grad = (prob * (prob_grad - delta_ref[group])).astype(jnp.bfloat16)
        value_part = contract(prob.astype(jnp.bfloat16), grad_rows, (1, 0))
        key_part = contract(score_grad, query_rows, (1, 0)) * softmax_scale
        query_part = contract(keys, score_grad, (0, 0))
        if query_in_ref is not None:
            query_part += query_in_ref[group]
        query_total_ref[group] = query_part
        kv_part_ref[0, group] = key_part.astype(kv_part_ref.dtype)
        kv_part_ref[1, group] = value_part.astype(kv_part_ref.dtype)


def tile_call(distance, starts, norms, deltas, queries, grads, kv, query_total=None):
    groups, cols, dim = queries.shape
    rows = kv.shape[2]
    args = [starts, norms, deltas, queries, grads, kv]
    aliases = {}
    if query_total is not None:
        aliases = {len(args): 0}
        args.append(query_total)
    whole = pl.BlockSpec(memory_space=pltpu.VMEM)
    return pl.pallas_call(
        functools.partial(tile_kernel, distance, 1.0 / math.sqrt(dim)),
        in_specs=[whole] * len(args),
        out_specs=(whole, whole),
        out_shape=(
            jax.ShapeDtypeStruct((groups, dim, cols), jnp.float32),
            jax.ShapeDtypeStruct(kv.shape, jnp.float32 if distance == 0 else jnp.bfloat16),
        ),
        input_output_aliases=aliases,
        compiler_params=pltpu.CompilerParams(vmem_limit_bytes=VMEM_LIMIT),
        cost_estimate=pl.CostEstimate(
            flops=WEIGHT * 10 * groups * cols * rows * dim,
            bytes_accessed=6 * groups * cols * dim,
            transcendentals=groups * cols * rows,
        ),
        name=f"tiles_{distance}",
    )(*args)


def query_kernel(softmax_scale, total_ref, out_ref):
    groups, heads, rows, _ = out_ref.shape

    def group_step(group, carry):
        for head in range(heads):
            part = total_ref[group, :, pl.ds(head * rows, rows)]
            out_ref[group, head] = (part.T * softmax_scale).astype(out_ref.dtype)
        return carry

    lax.fori_loop(0, groups, group_step, 0)


def query_call(query_total, rows):
    groups, dim, cols = query_total.shape
    whole = pl.BlockSpec(memory_space=pltpu.VMEM)
    return pl.pallas_call(
        functools.partial(query_kernel, 1.0 / math.sqrt(dim)),
        in_specs=[whole],
        out_specs=whole,
        out_shape=jax.ShapeDtypeStruct((groups, cols // rows, rows, dim), jnp.bfloat16),
        compiler_params=pltpu.CompilerParams(vmem_limit_bytes=VMEM_LIMIT),
        cost_estimate=pl.CostEstimate(
            flops=groups * cols * dim, bytes_accessed=6 * groups * cols * dim, transcendentals=0
        ),
        name="query_rows",
    )(query_total)


def sum_kernel(total_ref, part_ref, out_ref):
    out_ref[...] = total_ref[...] + part_ref[...].astype(jnp.float32)


def sum_call(total, part):
    whole = pl.BlockSpec(memory_space=pltpu.VMEM)
    return pl.pallas_call(
        sum_kernel,
        in_specs=[whole, whole],
        out_specs=whole,
        out_shape=jax.ShapeDtypeStruct(total.shape, total.dtype),
        input_output_aliases={0: 0},
        compiler_params=pltpu.CompilerParams(vmem_limit_bytes=VMEM_LIMIT),
        cost_estimate=pl.CostEstimate(flops=SUM_FLOPS, bytes_accessed=10 * total.size, transcendentals=0),
        name="kv_sum",
    )(total, part)


def last_kernel(total_ref, part_ref, key_ref, value_ref):
    for index, out_ref in enumerate((key_ref, value_ref)):
        whole = total_ref[index] + part_ref[index].astype(jnp.float32)
        out_ref[...] = jnp.transpose(whole, (1, 0, 2)).astype(out_ref.dtype)


def last_call(total, part):
    _, groups, rows, dim = total.shape
    whole = pl.BlockSpec(memory_space=pltpu.VMEM)
    out = jax.ShapeDtypeStruct((rows, groups, dim), jnp.bfloat16)
    return pl.pallas_call(
        last_kernel,
        in_specs=[whole, whole],
        out_specs=(whole, whole),
        out_shape=(out, out),
        compiler_params=pltpu.CompilerParams(vmem_limit_bytes=VMEM_LIMIT),
        cost_estimate=pl.CostEstimate(
            flops=total.size, bytes_accessed=8 * total.size, transcendentals=0
        ),
        name="kv_rows",
    )(total, part)


def shards(query_states, key_states, value_states, out_grad, log_norm, row_delta, doc_lengths):
    rows, heads, dim = query_states.shape
    group = heads // KV_HEADS
    reach = MOST // rows
    chunk = lax.axis_index("ctx") * lax.axis_size("head") + lax.axis_index("head")
    first_pos = chunk * rows

    kv = jnp.transpose(jnp.stack([key_states, value_states]), (0, 2, 1, 3))
    behind = {distance: chunk_shift(kv, distance) for distance in range(reach, 0, -1)}

    by_head = lambda x: jnp.transpose(x, (1, 0, 2)).reshape(KV_HEADS, group * rows, dim)
    queries, grads = by_head(query_states), by_head(out_grad)
    norms = (log_norm.T * LOG2E).reshape(KV_HEADS, 1, group * rows)
    deltas = row_delta.T.reshape(KV_HEADS, 1, group * rows)
    positions = first_pos + jnp.arange(rows, dtype=jnp.int32)
    starts = doc_starts(doc_lengths, positions) - first_pos
    starts = jnp.tile(starts, group).reshape(1, group * rows)

    rows_of = (starts, norms, deltas, queries, grads)
    query_total, kv_own = tile_call(0, *rows_of, kv)
    returned = []
    for distance in range(reach, 0, -1):
        query_total, kv_part = tile_call(distance, *rows_of, behind[distance], query_total)
        returned.append(chunk_shift(kv_part, -distance))
    query_heads = query_call(query_total, rows)
    for part in returned[:-1]:
        kv_own = sum_call(kv_own, part)
    key_grad, value_grad = last_call(kv_own, returned[-1])
    query_grad = jnp.transpose(query_heads.reshape(heads, rows, dim), (1, 0, 2))
    return (query_grad, key_grad, value_grad)


def solution(mesh):
    spec3 = P(("ctx", "head"), None, None)
    spec2 = P(("ctx", "head"), None)
    return jax.shard_map(
        shards,
        mesh=mesh,
        in_specs=(spec3, spec3, spec3, spec3, spec2, spec2, P()),
        out_specs=(spec3, spec3, spec3),
        check_vma=False,
    )
```

time: 77.2 us -> 61.3 us (0.79)
  the two profiles are of different devices: /device:TPU:253 before, /device:TPU:256 now
where the time goes in v2:
time: 61.3 us; the launch traced here: 60.8 us
  starting transfers between devices  29.1 us (47%)
  Pallas kernels  11.6 us (19%)
  waiting for transfers between devices  11.6 us (19%)
  local copies, waits for them, and re-layouts  4.99 us (8%)
  other arithmetic  2.7 us (4%)
  between operations  0.87 us (1%)
    ppermute x8, starting transfers between devices, chunk_shift(): return lax.ppermute(x, ('head', 'ctx'), pairs)  29.1 us
    ppermute x8, waiting for transfers between devices, chunk_shift(): return lax.ppermute(x, ('head', 'ctx'), pairs)  11.6 us
    pallas_call x5, Pallas kernels, tile_call(): pl.pallas_call(functools.partial(tile_kernel, distance, 1.0 / math.sqrt(d...  9.69 us
    transpose x2, local copies, waits for them, and re-layouts, shards(): jnp.transpose(x, (1, 0, 2)).reshape(KV_HEADS, group * rows, dim)  2.05 us
    reshape x1, local copies, waits for them, and re-layouts, shards(): query_grad = jnp.transpose(query_heads.reshape(heads, rows, dim), (1, 0, 2))  1.65 us
  transfers between devices with their start and end apart: 8, of which 3 were waited for; matrix products, arithmetic and copies ran while one was open for 11% of the time, Pallas kernels for 18%

profile of v2, /device:TPU:256, one launch (start us, length us, event | category | flops | bytes accessed | tf_op | source)
XLA Modules:
  0.0 60.8 jit_solution(3199710759665545616)
XLA Ops:
  0.6 0.0 copy-start.1
  0.6 1.1 %copy_bitcast_fusion.1 = (bf16[1,128,4,128]{3,1,2,0:T(8,128)(2,1)S(1)}, bf16[1,128,4,128]{3,1,2,0:T(8,128)(2,1)S(1)}) fusion(bf16[128,4,128]{2,1,0:T(4,128)(2,1)} %param.9, bf16[128,4,128]{2,1,0:T(4,128)(2,1)} %param.8), kind=kLoop, calls=%fused_computation.2 | loop fusion | bytes 524288 | tf_op jit(solution)/shard_map/stack | solution.py:184
  1.8 4.9 %collective-permute-start.3 = (bf16[2,4,128,128]{3,2,1,0:T(8,128)(2,1)S(1)}, bf16[2,4,128,128]{3,2,1,0:T(8,128)(2,1)S(1)}, u32[]{:S(2)}, u32[]{:S(2)}) collective-permute-start(bf16[2,4,128,128]{3,2,1,0:T(8,128)(2,1)S(1)} %maximum_bitcast_fusion.kv_ref), channel_id=1, source_target_pairs={{0,256},{64,320},{128,384},{192,448},{256,1},{320,65},{384,129},{4... | collective-permute-start | bytes 786440 | tf_op jit(solution)/shard_map/ppermute | solution.py:31
  6.7 3.5 %collective-permute-start.2 = (bf16[2,4,128,128]{3,2,1,0:T(8,128)(2,1)S(1)}, bf16[2,4,128,128]{3,2,1,0:T(8,128)(2,1)S(1)}, u32[]{:S(2)}, u32[]{:S(2)}) collective-permute-start(bf16[2,4,128,128]{3,2,1,0:T(8,128)(2,1)S(1)} %maximum_bitcast_fusion.kv_ref), channel_id=1, source_target_pairs={{0,192},{64,256},{128,320},{192,384},{256,448},{320,1},{384,65},{4... | collective-permute-start | bytes 786440 | tf_op jit(solution)/shard_map/ppermute | solution.py:31
  10.2 1.9 %collective-permute-start.1 = (bf16[2,4,128,128]{3,2,1,0:T(8,128)(2,1)S(1)}, bf16[2,4,128,128]{3,2,1,0:T(8,128)(2,1)S(1)}, u32[]{:S(2)}, u32[]{:S(2)}) collective-permute-start(bf16[2,4,128,128]{3,2,1,0:T(8,128)(2,1)S(1)} %maximum_bitcast_fusion.kv_ref), channel_id=1, source_target_pairs={{0,128},{64,192},{128,256},{192,320},{256,384},{320,448},{384,1},{... | collective-permute-start | bytes 786440 | tf_op jit(solution)/shard_map/ppermute | solution.py:31
  12.2 3.2 %collective-permute-start = (bf16[2,4,128,128]{3,2,1,0:T(8,128)(2,1)S(1)}, bf16[2,4,128,128]{3,2,1,0:T(8,128)(2,1)S(1)}, u32[]{:S(2)}, u32[]{:S(2)}) collective-permute-start(bf16[2,4,128,128]{3,2,1,0:T(8,128)(2,1)S(1)} %maximum_bitcast_fusion.kv_ref), channel_id=1, source_target_pairs={{0,64},{64,128},{128,192},{192,256},{256,320},{320,384},{384,448},... | collective-permute-start | bytes 786440 | tf_op jit(solution)/shard_map/ppermute | solution.py:31
  15.4 1.0 %reduce-window.9 = s32[2,128]{1,0:T(2,128)S(1)} reduce-window(s32[2,128]{1,0:T(2,128)} %bitcast.53, s32[]{:T(128)} %constant.7.clone.1), window={size=1x128 pad=0_0x127_0}, to_apply=%region_0.0 | reduce-window | flops 32512 | bytes 2052 | tf_op jit(solution)/shard_map/reduce-window
  16.4 0.1 slice.7
  16.5 0.1 slice_reduce_fusion
  16.6 0.1 add_bitcast_fusion
  16.7 0.7 %broadcast_multiply_fusion = f32[128,32]{0,1:T(8,128)S(1)} fusion(f32[128,32]{0,1:T(8,128)} %param.11), kind=kLoop, calls=%fused_computation.5 | loop fusion | flops 4096 | bytes 32768 | tf_op jit(solution)/shard_map/mul | solution.py:189
  17.4 0.8 %select_reduce_fusion = s32[128]{0:T(128)S(1)} fusion(s32[256]{0:T(256)} %param.13, s32[256]{0:T(256)S(1)} %add_bitcast_fusion, s32[128]{0:T(128)S(1)} %iota_add_fusion), kind=kLoop, calls=%fused_computation.4 | loop fusion | flops 98176 | bytes 3072 | tf_op jit(solution)/shard_map/reduce_sum | solution.py:23
  18.3 0.0 copy-start
  18.3 1.6 %copy.28 = bf16[32,128,128]{2,1,0:T(8,128)(2,1)S(1)} copy(bf16[32,128,128]{2,0,1:T(8,128)(2,1)} %bitcast.50) | data formatting | bytes 2097152 | tf_op jit(solution)/shard_map/transpose | solution.py:187
  19.9 0.0 copy-done.1
  19.9 0.4 copy.27
  20.3 0.0 copy-done
  20.4 1.8 %tiles_0.1 = (f32[4,128,1024]{2,1,0:T(8,128)S(1)}, f32[2,4,128,128]{3,2,1,0:T(8,128)S(1)}) custom-call(s32[1,1024]{1,0:T(1,128)S(1)} %bitcast.45, f32[4,1,1024]{2,1,0:T(1,128)S(1)} %bitcast.35, f32[4,1,1024]{2,1,0:T(1,128)S(1)} %bitcast.40, bf16[4,1024,128]{2,1,0:T(8,128)(2,1)S(1)} %bitcast.29, bf16[4,1024,128]{2,1,0:T(8,128)(2,1)S(1)} %bitcast.24, ...), custom_call_target="tpu_custom_call" | custom-call | flops 671088640 | bytes 3145728 | tf_op jit(solution)/shard_map/tiles_0/pallas_call | solution.py:89
  22.2 2.5 %collective-permute-done.3.kv_ref = bf16[2,4,128,128]{3,2,1,0:T(8,128)(2,1)S(1)} collective-permute-done((bf16[2,4,128,128]{3,2,1,0:T(8,128)(2,1)S(1)}, bf16[2,4,128,128]{3,2,1,0:T(8,128)(2,1)S(1)}, u32[]{:S(2)}, u32[]{:S(2)}) %collective-permute-start.3) | collective-permute-done | bytes 262176 | tf_op jit(solution)/shard_map/ppermute | solution.py:31
  24.7 2.0 %tiles_4.1 = (f32[4,128,1024]{2,1,0:T(8,128)S(1)}, bf16[2,4,128,128]{3,2,1,0:T(8,128)(2,1)S(1)}) custom-call(s32[1,1024]{1,0:T(1,128)S(1)} %bitcast.46, f32[4,1,1024]{2,1,0:T(1,128)S(1)} %bitcast.36, f32[4,1,1024]{2,1,0:T(1,128)S(1)} %bitcast.41, bf16[4,1024,128]{2,1,0:T(8,128)(2,1)S(1)} %bitcast.30, ...), custom_call_target="tpu_custom_call", output_to_operand_aliasing={{0}: (6, {})} | custom-call | flops 671088640 | bytes 3145728 | tf_op jit(solution)/shard_map/tiles_4/pallas_call | solution.py:89
  26.7 6.8 %collective-permute-start.4 = (bf16[2,4,128,128]{3,2,1,0:T(8,128)(2,1)S(1)}, bf16[2,4,128,128]{3,2,1,0:T(8,128)(2,1)S(1)}, u32[]{:S(2)}, u32[]{:S(2)}) collective-permute-start(bf16[2,4,128,128]{3,2,1,0:T(8,128)(2,1)S(1)} %get-tuple-element.21), channel_id=1, source_target_pairs={{256,0},{320,64},{384,128},{448,192},{1,256},{65,320},{129,384},{1... | collective-permute-start | bytes 786440 | tf_op jit(solution)/shard_map/ppermute | solution.py:31
  33.5 0.0 collective-permute-done.2.kv_ref
  33.5 2.0 %tiles_3.1 = (f32[4,128,1024]{2,1,0:T(8,128)S(1)}, bf16[2,4,128,128]{3,2,1,0:T(8,128)(2,1)S(1)}) custom-call(s32[1,1024]{1,0:T(1,128)S(1)} %bitcast.47, f32[4,1,1024]{2,1,0:T(1,128)S(1)} %bitcast.37, f32[4,1,1024]{2,1,0:T(1,128)S(1)} %bitcast.42, bf16[4,1024,128]{2,1,0:T(8,128)(2,1)S(1)} %bitcast.31, ...), custom_call_target="tpu_custom_call", output_to_operand_aliasing={{0}: (6, {})} | custom-call | flops 671088640 | bytes 3145728 | tf_op jit(solution)/shard_map/tiles_3/pallas_call | solution.py:89
  35.5 2.5 %collective-permute-start.5 = (bf16[2,4,128,128]{3,2,1,0:T(8,128)(2,1)S(1)}, bf16[2,4,128,128]{3,2,1,0:T(8,128)(2,1)S(1)}, u32[]{:S(2)}, u32[]{:S(2)}) collective-permute-start(bf16[2,4,128,128]{3,2,1,0:T(8,128)(2,1)S(1)} %get-tuple-element.22), channel_id=1, source_target_pairs={{192,0},{256,64},{320,128},{384,192},{448,256},{1,320},{65,384},{1... | collective-permute-start | bytes 786440 | tf_op jit(solution)/shard_map/ppermute | solution.py:31
  38.0 0.0 collective-permute-done.1.kv_ref
  38.0 2.0 %tiles_2.1 = (f32[4,128,1024]{2,1,0:T(8,128)S(1)}, bf16[2,4,128,128]{3,2,1,0:T(8,128)(2,1)S(1)}) custom-call(s32[1,1024]{1,0:T(1,128)S(1)} %bitcast.48, f32[4,1,1024]{2,1,0:T(1,128)S(1)} %bitcast.38, f32[4,1,1024]{2,1,0:T(1,128)S(1)} %bitcast.43, bf16[4,1024,128]{2,1,0:T(8,128)(2,1)S(1)} %bitcast.32, ...), custom_call_target="tpu_custom_call", output_to_operand_aliasing={{0}: (6, {})} | custom-call | flops 671088640 | bytes 3145728 | tf_op jit(solution)/shard_map/tiles_2/pallas_call | solution.py:89
  39.9 4.3 %collective-permute-start.6 = (bf16[2,4,128,128]{3,2,1,0:T(8,128)(2,1)S(1)}, bf16[2,4,128,128]{3,2,1,0:T(8,128)(2,1)S(1)}, u32[]{:S(2)}, u32[]{:S(2)}) collective-permute-start(bf16[2,4,128,128]{3,2,1,0:T(8,128)(2,1)S(1)} %get-tuple-element.23), channel_id=1, source_target_pairs={{128,0},{192,64},{256,128},{320,192},{384,256},{448,320},{1,384},{... | collective-permute-start | bytes 786440 | tf_op jit(solution)/shard_map/ppermute | solution.py:31
  44.2 0.0 collective-permute-done.kv_ref
  44.2 2.0 %tiles_1.1 = (f32[4,128,1024]{2,1,0:T(8,128)S(1)}, bf16[2,4,128,128]{3,2,1,0:T(8,128)(2,1)S(1)}) custom-call(s32[1,1024]{1,0:T(1,128)S(1)} %bitcast.49, f32[4,1,1024]{2,1,0:T(1,128)S(1)} %bitcast.39, f32[4,1,1024]{2,1,0:T(1,128)S(1)} %bitcast.44, bf16[4,1024,128]{2,1,0:T(8,128)(2,1)S(1)} %bitcast.33, ...), custom_call_target="tpu_custom_call", output_to_operand_aliasing={{0}: (6, {})} | custom-call | flops 671088640 | bytes 3145728 | tf_op jit(solution)/shard_map/tiles_1/pallas_call | solution.py:89
  46.2 1.9 %collective-permute-start.7 = (bf16[2,4,128,128]{3,2,1,0:T(8,128)(2,1)S(1)}, bf16[2,4,128,128]{3,2,1,0:T(8,128)(2,1)S(1)}, u32[]{:S(2)}, u32[]{:S(2)}) collective-permute-start(bf16[2,4,128,128]{3,2,1,0:T(8,128)(2,1)S(1)} %get-tuple-element.24), channel_id=1, source_target_pairs={{64,0},{128,64},{192,128},{256,192},{320,256},{384,320},{448,384},... | collective-permute-start | bytes 786440 | tf_op jit(solution)/shard_map/ppermute | solution.py:31
  48.1 0.8 %query_rows.1 = bf16[4,8,128,128]{3,2,1,0:T(8,128)(2,1)S(1)} custom-call(f32[4,128,1024]{2,1,0:T(8,128)S(1)} %get-tuple-element.19.total_ref), custom_call_target="tpu_custom_call" | custom-call | flops 524288 | bytes 3145728 | tf_op jit(solution)/shard_map/query_rows/pallas_call | solution.py:123
  49.0 1.6 %copy.35 = bf16[32,128,128]{2,0,1:T(8,128)(2,1)} copy(bf16[32,128,128]{2,1,0:T(8,128)(2,1)S(1)} %bitcast.34) | data formatting | bytes 2097152 | tf_op jit(solution)/shard_map/reshape | solution.py:205
  50.6 0.0 collective-permute-done.4.part_ref
  50.6 0.1 kv_sum.3.total_ref
  50.7 0.0 collective-permute-done.5.part_ref
  50.7 0.1 kv_sum.4.total_ref
  50.8 1.2 %collective-permute-done.6.part_ref = bf16[2,4,128,128]{3,2,1,0:T(8,128)(2,1)S(1)} collective-permute-done((bf16[2,4,128,128]{3,2,1,0:T(8,128)(2,1)S(1)}, bf16[2,4,128,128]{3,2,1,0:T(8,128)(2,1)S(1)}, u32[]{:S(2)}, u32[]{:S(2)}) %collective-permute-start.6) | collective-permute-done | bytes 262176 | tf_op jit(solution)/shard_map/ppermute | solution.py:31
  52.0 0.1 kv_sum.5.total_ref
  52.1 7.9 %collective-permute-done.7.part_ref = bf16[2,4,128,128]{3,2,1,0:T(8,128)(2,1)S(1)} collective-permute-done((bf16[2,4,128,128]{3,2,1,0:T(8,128)(2,1)S(1)}, bf16[2,4,128,128]{3,2,1,0:T(8,128)(2,1)S(1)}, u32[]{:S(2)}, u32[]{:S(2)}) %collective-permute-start.7) | collective-permute-done | bytes 262176 | tf_op jit(solution)/shard_map/ppermute | solution.py:31
  60.0 0.8 %kv_rows.1 = (bf16[128,4,128]{2,1,0:T(4,128)(2,1)}, bf16[128,4,128]{2,1,0:T(4,128)(2,1)}) custom-call(f32[2,4,128,128]{3,2,1,0:T(8,128)S(1)} %kv_sum.5.total_ref, bf16[2,4,128,128]{3,2,1,0:T(8,128)(2,1)S(1)} %collective-permute-done.7.part_ref), custom_call_target="tpu_custom_call" | custom-call | flops 131072 | bytes 1048576 | tf_op jit(solution)/shard_map/kv_rows/pallas_call | solution.py:164
  (5 shorter events, 0.1 us)
Async XLA Ops:
  0.6 19.3 %copy-start.1 = (bf16[128,32,128]{2,1,0:T(8,128)(2,1)S(1)}, bf16[128,32,128]{2,1,0:T(8,128)(2,1)}, u32[]{:S(2)}) copy-start(bf16[128,32,128]{2,1,0:T(8,128)(2,1)} %param.7) | copy-start | bytes 3145732
  1.8 22.9 %collective-permute-start.3 = (bf16[2,4,128,128]{3,2,1,0:T(8,128)(2,1)S(1)}, bf16[2,4,128,128]{3,2,1,0:T(8,128)(2,1)S(1)}, u32[]{:S(2)}, u32[]{:S(2)}) collective-permute-start(bf16[2,4,128,128]{3,2,1,0:T(8,128)(2,1)S(1)} %maximum_bitcast_fusion.kv_ref), channel_id=1, source_target_pairs={{0,256},{64,320},{128,384},{192,448},{256,1},{320,65},{384,129},{4... | collective-permute-start | bytes 786440 | tf_op jit(solution)/shard_map/ppermute | solution.py:31
  6.7 26.8 %collective-permute-start.2 = (bf16[2,4,128,128]{3,2,1,0:T(8,128)(2,1)S(1)}, bf16[2,4,128,128]{3,2,1,0:T(8,128)(2,1)S(1)}, u32[]{:S(2)}, u32[]{:S(2)}) collective-permute-start(bf16[2,4,128,128]{3,2,1,0:T(8,128)(2,1)S(1)} %maximum_bitcast_fusion.kv_ref), channel_id=1, source_target_pairs={{0,192},{64,256},{128,320},{192,384},{256,448},{320,1},{384,65},{4... | collective-permute-start | bytes 786440 | tf_op jit(solution)/shard_map/ppermute | solution.py:31
  10.2 27.7 %collective-permute-start.1 = (bf16[2,4,128,128]{3,2,1,0:T(8,128)(2,1)S(1)}, bf16[2,4,128,128]{3,2,1,0:T(8,128)(2,1)S(1)}, u32[]{:S(2)}, u32[]{:S(2)}) collective-permute-start(bf16[2,4,128,128]{3,2,1,0:T(8,128)(2,1)S(1)} %maximum_bitcast_fusion.kv_ref), channel_id=1, source_target_pairs={{0,128},{64,192},{128,256},{192,320},{256,384},{320,448},{384,1},{... | collective-permute-start | bytes 786440 | tf_op jit(solution)/shard_map/ppermute | solution.py:31
  12.2 32.1 %collective-permute-start = (bf16[2,4,128,128]{3,2,1,0:T(8,128)(2,1)S(1)}, bf16[2,4,128,128]{3,2,1,0:T(8,128)(2,1)S(1)}, u32[]{:S(2)}, u32[]{:S(2)}) collective-permute-start(bf16[2,4,128,128]{3,2,1,0:T(8,128)(2,1)S(1)} %maximum_bitcast_fusion.kv_ref), channel_id=1, source_target_pairs={{0,64},{64,128},{128,192},{192,256},{256,320},{320,384},{384,448},... | collective-permute-start | bytes 786440 | tf_op jit(solution)/shard_map/ppermute | solution.py:31
  18.3 2.1 %copy-start = (f32[128,32]{0,1:T(8,128)S(1)}, f32[128,32]{0,1:T(8,128)}, u32[]{:S(2)}) copy-start(f32[128,32]{0,1:T(8,128)} %param.12) | copy-start | bytes 49156
  26.7 24.0 %collective-permute-start.4 = (bf16[2,4,128,128]{3,2,1,0:T(8,128)(2,1)S(1)}, bf16[2,4,128,128]{3,2,1,0:T(8,128)(2,1)S(1)}, u32[]{:S(2)}, u32[]{:S(2)}) collective-permute-start(bf16[2,4,128,128]{3,2,1,0:T(8,128)(2,1)S(1)} %get-tuple-element.21), channel_id=1, source_target_pairs={{256,0},{320,64},{384,128},{448,192},{1,256},{65,320},{129,384},{1... | collective-permute-start | bytes 786440 | tf_op jit(solution)/shard_map/ppermute | solution.py:31
  35.5 15.3 %collective-permute-start.5 = (bf16[2,4,128,128]{3,2,1,0:T(8,128)(2,1)S(1)}, bf16[2,4,128,128]{3,2,1,0:T(8,128)(2,1)S(1)}, u32[]{:S(2)}, u32[]{:S(2)}) collective-permute-start(bf16[2,4,128,128]{3,2,1,0:T(8,128)(2,1)S(1)} %get-tuple-element.22), channel_id=1, source_target_pairs={{192,0},{256,64},{320,128},{384,192},{448,256},{1,320},{65,384},{1... | collective-permute-start | bytes 786440 | tf_op jit(solution)/shard_map/ppermute | solution.py:31
  39.9 12.1 %collective-permute-start.6 = (bf16[2,4,128,128]{3,2,1,0:T(8,128)(2,1)S(1)}, bf16[2,4,128,128]{3,2,1,0:T(8,128)(2,1)S(1)}, u32[]{:S(2)}, u32[]{:S(2)}) collective-permute-start(bf16[2,4,128,128]{3,2,1,0:T(8,128)(2,1)S(1)} %get-tuple-element.23), channel_id=1, source_target_pairs={{128,0},{192,64},{256,128},{320,192},{384,256},{448,320},{1,384},{... | collective-permute-start | bytes 786440 | tf_op jit(solution)/shard_map/ppermute | solution.py:31
  46.2 13.8 %collective-permute-start.7 = (bf16[2,4,128,128]{3,2,1,0:T(8,128)(2,1)S(1)}, bf16[2,4,128,128]{3,2,1,0:T(8,128)(2,1)S(1)}, u32[]{:S(2)}, u32[]{:S(2)}) collective-permute-start(bf16[2,4,128,128]{3,2,1,0:T(8,128)(2,1)S(1)} %get-tuple-element.24), channel_id=1, source_target_pairs={{64,0},{128,64},{192,128},{256,192},{320,256},{384,320},{448,384},... | collective-permute-start | bytes 786440 | tf_op jit(solution)/shard_map/ppermute | solution.py:31

commit v3 on v2

--- a/solution.py
+++ b/solution.py
@@ -13,21 +13,16 @@
 MOST = 512
 LOG2E = 1.4426950408889634
 VMEM_LIMIT = 40 * 1024 * 1024
-WEIGHT = 1
-SUM_FLOPS = 5_000_000_000
-
-
-def doc_starts(doc_lengths, positions):
-    doc_ends = jnp.cumsum(doc_lengths)
-    before = jnp.where(doc_ends[None, :] <= positions[:, None], doc_lengths[None, :], 0)
-    return jnp.sum(before, axis=1)
-
-
-def chunk_shift(x, by):
+SUM_FLOPS = 700_000_000
+ORDER = (3, 4, 2, 1)
+
+
+def chunk_permute(x, target):
     heads, ctxs = lax.axis_size("head"), lax.axis_size("ctx")
     count = heads * ctxs
     place = lambda c: (c % heads) * ctxs + c // heads
-    pairs = [(place(c), place(c + by)) for c in range(count) if 0 <= c + by < count]
+    routes = [(c, target(c)) for c in range(count)]
+    pairs = [(place(c), place(to)) for c, to in routes if 0 <= to < count]
     return lax.ppermute(x, ("head", "ctx"), pairs)
 
 
@@ -37,8 +32,48 @@
     )
 
 
+def rows_kernel(place_ref, norm_ref, delta_ref, length_ref, start_ref, norm_out, delta_out):
+    groups, _, cols = norm_out.shape
+    heads, rows = norm_ref.shape
+    docs = length_ref.shape[1]
+    norms = norm_ref[...] * LOG2E
+    deltas = delta_ref[...]
+    for head in range(heads):
+        group, at = divmod(head * rows, cols)
+        norm_out[group, :, pl.ds(at, rows)] = norms[head : head + 1]
+        delta_out[group, :, pl.ds(at, rows)] = deltas[head : head + 1]
+    upto = lax.broadcasted_iota(jnp.int32, (docs, docs), 1) <= lax.broadcasted_iota(
+        jnp.int32, (docs, docs), 0
+    )
+    lengths = length_ref[...].astype(jnp.float32)
+    ends = jnp.sum(jnp.where(upto, lengths, 0.0), axis=1, keepdims=True)
+    first = place_ref[0]
+    positions = (lax.broadcasted_iota(jnp.int32, (docs, rows), 1) + first).astype(jnp.float32)
+    starts = jnp.max(jnp.where(ends <= positions, ends, 0.0), axis=0, keepdims=True)
+    starts = starts.astype(jnp.int32) - first
+    for slot in range(start_ref.shape[0]):
+        for at in range(0, cols, rows):
+            start_ref[slot, :, pl.ds(at, rows)] = starts + place_ref[1 + slot]
+
+
+def rows_call(place, log_norm, row_delta, doc_lengths):
+    rows, heads = log_norm.shape
+    cols = heads * rows // KV_HEADS
+    whole = pl.BlockSpec(memory_space=pltpu.VMEM)
+    slots = place.shape[0] - 1
+    wide = jax.ShapeDtypeStruct((KV_HEADS, 1, cols), jnp.float32)
+    return pl.pallas_call(
+        rows_kernel,
+        in_specs=[pl.BlockSpec(memory_space=pltpu.SMEM), whole, whole, whole],
+        out_specs=(whole, whole, whole),
+        out_shape=(jax.ShapeDtypeStruct((slots, 1, cols), jnp.int32), wide, wide),
+        compiler_params=pltpu.CompilerParams(vmem_limit_bytes=VMEM_LIMIT),
+        name="row_terms",
+    )(place, log_norm.T, row_delta.T, doc_lengths.reshape(1, -1))
+
+
 def tile_kernel(
-    distance,
+    slot,
     softmax_scale,
     start_ref,
     norm_ref,
@@ -52,32 +87,47 @@
     query_total_ref, kv_part_ref = rest[-2:]
     groups, cols, _ = query_ref.shape
     rows = kv_ref.shape[2]
-    key_pos = lax.broadcasted_iota(jnp.int32, (rows, cols), 0) - distance * rows
-    allowed = key_pos >= start_ref[...]
-    if distance == 0:
-        query_pos = lax.broadcasted_iota(jnp.int32, (rows, cols), 1) & (rows - 1)
-        allowed = allowed & (key_pos <= query_pos)
-    for group in range(groups):
-        keys = kv_ref[0, group]
-        values = kv_ref[1, group]
-        query_rows = query_ref[group]
-        grad_rows = grad_ref[group]
-        scores = contract(keys, query_rows, (1, 1))
-        prob_grad = contract(values, grad_rows, (1, 1))
-        prob = jnp.exp2(scores * (softmax_scale * LOG2E) - norm_ref[group])
-        prob = jnp.where(allowed, prob, 0.0)
-        score_grad = (prob * (prob_grad - delta_ref[group])).astype(jnp.bfloat16)
-        value_part = contract(prob.astype(jnp.bfloat16), grad_rows, (1, 0))
-        key_part = contract(score_grad, query_rows, (1, 0)) * softmax_scale
-        query_part = contract(keys, score_grad, (0, 0))
-        if query_in_ref is not None:
-            query_part += query_in_ref[group]
-        query_total_ref[group] = query_part
-        kv_part_ref[0, group] = key_part.astype(kv_part_ref.dtype)
-        kv_part_ref[1, group] = value_part.astype(kv_part_ref.dtype)
-
-
-def tile_call(distance, starts, norms, deltas, queries, grads, kv, query_total=None):
+    def work():
+        key_pos = lax.broadcasted_iota(jnp.int32, (rows, cols), 0)
+        allowed = key_pos >= start_ref[slot]
+        if slot == 0:
+            query_pos = lax.broadcasted_iota(jnp.int32, (rows, cols), 1) & (rows - 1)
+            allowed = allowed & (key_pos <= query_pos)
+        for group in range(groups):
+            keys = kv_ref[0, group]
+            values = kv_ref[1, group]
+            query_rows = query_ref[group]
+            grad_rows = grad_ref[group]
+            scores = contract(keys, query_rows, (1, 1))
+            prob_grad = contract(values, grad_rows, (1, 1))
+            prob = jnp.exp2(scores * (softmax_scale * LOG2E) - norm_ref[group])
+            prob = jnp.where(allowed, prob, 0.0)
+            score_grad = (prob * (prob_grad - delta_ref[group])).astype(jnp.bfloat16)
+            value_part = contract(prob.astype(jnp.bfloat16), grad_rows, (1, 0))
+            key_part = contract(score_grad, query_rows, (1, 0)) * softmax_scale
+            query_part = contract(keys, score_grad, (0, 0))
+            if query_in_ref is not None:
+                query_part += query_in_ref[group]
+            query_total_ref[group] = query_part
+            kv_part_ref[0, group] = key_part.astype(kv_part_ref.dtype)
+            kv_part_ref[1, group] = value_part.astype(kv_part_ref.dtype)
+
+    if slot == 0:
+        work()
+        return
+    needed = jnp.min(start_ref[slot, :, pl.ds(0, rows)]) < rows
+    pl.when(needed)(work)
+
+    @pl.when(jnp.logical_not(needed))
+    def _():
+        if query_in_ref is None:
+            query_total_ref[...] = jnp.zeros_like(query_total_ref)
+        else:
+            query_total_ref[...] = query_in_ref[...]
+        kv_part_ref[...] = jnp.zeros_like(kv_part_ref)
+
+
+def tile_call(slot, starts, norms, deltas, queries, grads, kv, query_total=None):
     groups, cols, dim = queries.shape
     rows = kv.shape[2]
     args = [starts, norms, deltas, queries, grads, kv]
@@ -87,21 +137,21 @@
         args.append(query_total)
     whole = pl.BlockSpec(memory_space=pltpu.VMEM)
     return pl.pallas_call(
-        functools.partial(tile_kernel, distance, 1.0 / math.sqrt(dim)),
+        functools.partial(tile_kernel, slot, 1.0 / math.sqrt(dim)),
         in_specs=[whole] * len(args),
         out_specs=(whole, whole),
         out_shape=(
             jax.ShapeDtypeStruct((groups, dim, cols), jnp.float32),
-            jax.ShapeDtypeStruct(kv.shape, jnp.float32 if distance == 0 else jnp.bfloat16),
+            jax.ShapeDtypeStruct(kv.shape, jnp.float32 if slot == 0 else jnp.bfloat16),
         ),
         input_output_aliases=aliases,
         compiler_params=pltpu.CompilerParams(vmem_limit_bytes=VMEM_LIMIT),
         cost_estimate=pl.CostEstimate(
-            flops=WEIGHT * 10 * groups * cols * rows * dim,
+            flops=10 * groups * cols * rows * dim,
             bytes_accessed=6 * groups * cols * dim,
             transcendentals=groups * cols * rows,
         ),
-        name=f"tiles_{distance}",
+        name=f"tiles_{slot}",
     )(*args)
 
 
@@ -177,27 +227,25 @@
 def shards(query_states, key_states, value_states, out_grad, log_norm, row_delta, doc_lengths):
     rows, heads, dim = query_states.shape
     group = heads // KV_HEADS
-    reach = MOST // rows
     chunk = lax.axis_index("ctx") * lax.axis_size("head") + lax.axis_index("head")
     first_pos = chunk * rows
 
     kv = jnp.transpose(jnp.stack([key_states, value_states]), (0, 2, 1, 3))
-    behind = {distance: chunk_shift(kv, distance) for distance in range(reach, 0, -1)}
+    behind = {distance: chunk_permute(kv, lambda c, d=distance: c + d) for distance in ORDER}
 
     by_head = lambda x: jnp.transpose(x, (1, 0, 2)).reshape(KV_HEADS, group * rows, dim)
     queries, grads = by_head(query_states), by_head(out_grad)
-    norms = (log_norm.T * LOG2E).reshape(KV_HEADS, 1, group * rows)
-    deltas = row_delta.T.reshape(KV_HEADS, 1, group * rows)
-    positions = first_pos + jnp.arange(rows, dtype=jnp.int32)
-    starts = doc_starts(doc_lengths, positions) - first_pos
-    starts = jnp.tile(starts, group).reshape(1, group * rows)
+    distances = jnp.asarray((0, *ORDER), jnp.int32)
+    place = jnp.concatenate([jnp.reshape(first_pos, (1,)), distances * rows])
+    starts, norms, deltas = rows_call(place, log_norm, row_delta, doc_lengths)
 
     rows_of = (starts, norms, deltas, queries, grads)
-    query_total, kv_own = tile_call(0, *rows_of, kv)
+    query_total = None
     returned = []
-    for distance in range(reach, 0, -1):
-        query_total, kv_part = tile_call(distance, *rows_of, behind[distance], query_total)
-        returned.append(chunk_shift(kv_part, -distance))
+    for slot, distance in enumerate(ORDER, 1):
+        query_total, kv_part = tile_call(slot, *rows_of, behind[distance], query_total)
+        returned.append(chunk_permute(kv_part, lambda c, d=distance: c - d))
+    query_total, kv_own = tile_call(0, *rows_of, kv, query_total)
     query_heads = query_call(query_total, rows)
     for part in returned[:-1]:
         kv_own = sum_call(kv_own, part)

time: 61.3 us -> 55.9 us (0.912)
  the two profiles are of different devices: /device:TPU:256 before, /device:TPU:321 now
where the time goes in v3:
time: 55.9 us; the launch traced here: 55.6 us
  starting transfers between devices  39.2 us (70%)
  Pallas kernels  8.22 us (15%)
  local copies, waits for them, and re-layouts  4.81 us (9%)
  waiting for transfers between devices  2.34 us (4%)
  between operations  0.91 us (2%)
    ppermute x8, starting transfers between devices, chunk_permute(): return lax.ppermute(x, ('head', 'ctx'), pairs)  39.2 us
    pallas_call x5, Pallas kernels, tile_call(): pl.pallas_call(functools.partial(tile_kernel, slot, 1.0 / math.sqrt(dim))...  5.61 us
    ppermute x8, waiting for transfers between devices, chunk_permute(): return lax.ppermute(x, ('head', 'ctx'), pairs)  2.34 us
    transpose x2, local copies, waits for them, and re-layouts, shards(): jnp.transpose(x, (1, 0, 2)).reshape(KV_HEADS, group * rows, dim)  2.12 us
    reshape x1, local copies, waits for them, and re-layouts, shards(): query_grad = jnp.transpose(query_heads.reshape(heads, rows, dim), (1, 0, 2))  1.65 us
  transfers between devices with their start and end apart: 8, of which 1 were waited for; matrix products, arithmetic and copies ran while one was open for 7% of the time, Pallas kernels for 13%

profile of v3, /device:TPU:321, one launch (start us, length us, event | category | flops | bytes accessed | tf_op | source)
XLA Modules:
  0.0 55.6 jit_solution(13400828514570666392)
XLA Ops:
  0.6 1.0 %copy_bitcast_fusion.1 = (bf16[1,128,4,128]{3,1,2,0:T(8,128)(2,1)S(1)}, bf16[1,128,4,128]{3,1,2,0:T(8,128)(2,1)S(1)}) fusion(bf16[128,4,128]{2,1,0:T(4,128)(2,1)} %param.10, bf16[128,4,128]{2,1,0:T(4,128)(2,1)} %param.9), kind=kLoop, calls=%fused_computation.2 | loop fusion | bytes 524288 | tf_op jit(solution)/shard_map/stack | solution.py:233
  1.7 4.1 %collective-permute-start.3 = (bf16[2,4,128,128]{3,2,1,0:T(8,128)(2,1)S(1)}, bf16[2,4,128,128]{3,2,1,0:T(8,128)(2,1)S(1)}, u32[]{:S(2)}, u32[]{:S(2)}) collective-permute-start(bf16[2,4,128,128]{3,2,1,0:T(8,128)(2,1)S(1)} %maximum_bitcast_fusion.kv_ref), channel_id=1, source_target_pairs={{0,192},{64,256},{128,320},{192,384},{256,448},{320,1},{384,65},{4... | collective-permute-start | bytes 786440 | tf_op jit(solution)/shard_map/ppermute | solution.py:26
  5.8 4.4 %collective-permute-start.2 = (bf16[2,4,128,128]{3,2,1,0:T(8,128)(2,1)S(1)}, bf16[2,4,128,128]{3,2,1,0:T(8,128)(2,1)S(1)}, u32[]{:S(2)}, u32[]{:S(2)}) collective-permute-start(bf16[2,4,128,128]{3,2,1,0:T(8,128)(2,1)S(1)} %maximum_bitcast_fusion.kv_ref), channel_id=1, source_target_pairs={{0,256},{64,320},{128,384},{192,448},{256,1},{320,65},{384,129},{4... | collective-permute-start | bytes 786440 | tf_op jit(solution)/shard_map/ppermute | solution.py:26
  10.2 4.1 %collective-permute-start.1 = (bf16[2,4,128,128]{3,2,1,0:T(8,128)(2,1)S(1)}, bf16[2,4,128,128]{3,2,1,0:T(8,128)(2,1)S(1)}, u32[]{:S(2)}, u32[]{:S(2)}) collective-permute-start(bf16[2,4,128,128]{3,2,1,0:T(8,128)(2,1)S(1)} %maximum_bitcast_fusion.kv_ref), channel_id=1, source_target_pairs={{0,128},{64,192},{128,256},{192,320},{256,384},{320,448},{384,1},{... | collective-permute-start | bytes 786440 | tf_op jit(solution)/shard_map/ppermute | solution.py:26
  14.3 2.1 %collective-permute-start = (bf16[2,4,128,128]{3,2,1,0:T(8,128)(2,1)S(1)}, bf16[2,4,128,128]{3,2,1,0:T(8,128)(2,1)S(1)}, u32[]{:S(2)}, u32[]{:S(2)}) collective-permute-start(bf16[2,4,128,128]{3,2,1,0:T(8,128)(2,1)S(1)} %maximum_bitcast_fusion.kv_ref), channel_id=1, source_target_pairs={{0,64},{64,128},{128,192},{192,256},{256,320},{320,384},{384,448},... | collective-permute-start | bytes 786440 | tf_op jit(solution)/shard_map/ppermute | solution.py:26
  16.4 0.0 copy-start.3
  16.4 0.0 copy-start.4
  16.4 0.0 copy-start
  16.4 0.0 copy-start.1
  16.4 0.0 copy-start.2
  16.5 1.7 %copy.18 = bf16[32,128,128]{2,1,0:T(8,128)(2,1)S(1)} copy(bf16[32,128,128]{2,0,1:T(8,128)(2,1)} %bitcast.32) | data formatting | bytes 2097152 | tf_op jit(solution)/shard_map/transpose | solution.py:236
  18.2 0.0 copy-done.3
  18.2 0.4 copy.19
  18.6 0.0 copy-done.4
  18.6 0.1 pad_add_fusion.place_ref
  18.7 0.0 copy-done
  18.7 0.0 copy-done.1
  18.7 0.0 copy-done.2
  18.7 0.7 %row_terms.1 = (s32[5,1,1024]{2,1,0:T(1,128)S(1)}, f32[4,1,1024]{2,1,0:T(1,128)S(1)}, f32[4,1,1024]{2,1,0:T(1,128)S(1)}) custom-call(s32[6]{0:T(128)S(1)} %pad_add_fusion.place_ref, f32[32,128]{1,0:T(8,128)S(1)} %bitcast.29, f32[32,128]{1,0:T(8,128)S(1)} %bitcast.30, s32[1,256]{1,0:T(1,128)S(1)} %bitcast.31), custom_call_target="tpu_custom_call" | custom-call | tf_op jit(solution)/shard_map/row_terms/pallas_call | solution.py:65
  19.4 0.0 collective-permute-done.3.kv_ref
  19.4 0.4 tiles_1.1
  19.8 6.4 %collective-permute-start.4 = (bf16[2,4,128,128]{3,2,1,0:T(8,128)(2,1)S(1)}, bf16[2,4,128,128]{3,2,1,0:T(8,128)(2,1)S(1)}, u32[]{:S(2)}, u32[]{:S(2)}) collective-permute-start(bf16[2,4,128,128]{3,2,1,0:T(8,128)(2,1)S(1)} %get-tuple-element.27), channel_id=1, source_target_pairs={{192,0},{256,64},{320,128},{384,192},{448,256},{1,320},{65,384},{1... | collective-permute-start | bytes 786440 | tf_op jit(solution)/shard_map/ppermute | solution.py:26
  26.1 0.0 collective-permute-done.2.kv_ref
  26.2 0.5 tiles_2.1
  26.7 8.2 %collective-permute-start.5 = (bf16[2,4,128,128]{3,2,1,0:T(8,128)(2,1)S(1)}, bf16[2,4,128,128]{3,2,1,0:T(8,128)(2,1)S(1)}, u32[]{:S(2)}, u32[]{:S(2)}) collective-permute-start(bf16[2,4,128,128]{3,2,1,0:T(8,128)(2,1)S(1)} %get-tuple-element.28), channel_id=1, source_target_pairs={{256,0},{320,64},{384,128},{448,192},{1,256},{65,320},{129,384},{1... | collective-permute-start | bytes 786440 | tf_op jit(solution)/shard_map/ppermute | solution.py:26
  34.8 0.0 collective-permute-done.1.kv_ref
  34.8 0.5 tiles_3.1
  35.4 7.9 %collective-permute-start.6 = (bf16[2,4,128,128]{3,2,1,0:T(8,128)(2,1)S(1)}, bf16[2,4,128,128]{3,2,1,0:T(8,128)(2,1)S(1)}, u32[]{:S(2)}, u32[]{:S(2)}) collective-permute-start(bf16[2,4,128,128]{3,2,1,0:T(8,128)(2,1)S(1)} %get-tuple-element.29), channel_id=1, source_target_pairs={{128,0},{192,64},{256,128},{320,192},{384,256},{448,320},{1,384},{... | collective-permute-start | bytes 786440 | tf_op jit(solution)/shard_map/ppermute | solution.py:26
  43.3 0.0 collective-permute-done.kv_ref
  43.3 2.2 %tiles_4.1 = (f32[4,128,1024]{2,1,0:T(8,128)S(1)}, bf16[2,4,128,128]{3,2,1,0:T(8,128)(2,1)S(1)}) custom-call(s32[5,1,1024]{2,1,0:T(1,128)S(1)} %get-tuple-element.18.start_ref, f32[4,1,1024]{2,1,0:T(1,128)S(1)} %get-tuple-element.19.norm_ref, f32[4,1,1024]{2,1,0:T(1,128)S(1)} %get-tuple-element.20.delta_ref, ...), custom_call_target="tpu_custom_call", output_to_operand_aliasing={{0}: (6, {})} | custom-call | flops 671088640 | bytes 3145728 | tf_op jit(solution)/shard_map/tiles_4/pallas_call | solution.py:139
  45.4 2.1 %collective-permute-start.7 = (bf16[2,4,128,128]{3,2,1,0:T(8,128)(2,1)S(1)}, bf16[2,4,128,128]{3,2,1,0:T(8,128)(2,1)S(1)}, u32[]{:S(2)}, u32[]{:S(2)}) collective-permute-start(bf16[2,4,128,128]{3,2,1,0:T(8,128)(2,1)S(1)} %get-tuple-element.30), channel_id=1, source_target_pairs={{64,0},{128,64},{192,128},{256,192},{320,256},{384,320},{448,384},... | collective-permute-start | bytes 786440 | tf_op jit(solution)/shard_map/ppermute | solution.py:26
  47.5 2.1 %tiles_0.1 = (f32[4,128,1024]{2,1,0:T(8,128)S(1)}, f32[2,4,128,128]{3,2,1,0:T(8,128)S(1)}) custom-call(s32[5,1,1024]{2,1,0:T(1,128)S(1)} %get-tuple-element.18.start_ref, f32[4,1,1024]{2,1,0:T(1,128)S(1)} %get-tuple-element.19.norm_ref, f32[4,1,1024]{2,1,0:T(1,128)S(1)} %get-tuple-element.20.delta_ref, ...), custom_call_target="tpu_custom_call", output_to_operand_aliasing={{0}: (6, {})} | custom-call | flops 671088640 | bytes 3145728 | tf_op jit(solution)/shard_map/tiles_0/pallas_call | solution.py:139
  49.6 0.8 %query_rows.1 = bf16[4,8,128,128]{3,2,1,0:T(8,128)(2,1)S(1)} custom-call(f32[4,128,1024]{2,1,0:T(8,128)S(1)} %get-tuple-element.25.total_ref), custom_call_target="tpu_custom_call" | custom-call | flops 524288 | bytes 3145728 | tf_op jit(solution)/shard_map/query_rows/pallas_call | solution.py:173
  50.4 1.6 %copy.26 = bf16[32,128,128]{2,0,1:T(8,128)(2,1)} copy(bf16[32,128,128]{2,1,0:T(8,128)(2,1)S(1)} %bitcast.28) | data formatting | bytes 2097152 | tf_op jit(solution)/shard_map/reshape | solution.py:253
  52.1 0.0 collective-permute-done.4.part_ref
  52.1 0.1 kv_sum.3.total_ref
  52.2 0.0 collective-permute-done.5.part_ref
  52.2 0.1 kv_sum.4.total_ref
  52.3 0.0 collective-permute-done.6.part_ref
  52.3 0.1 kv_sum.5.total_ref
  52.4 2.3 %collective-permute-done.7.part_ref = bf16[2,4,128,128]{3,2,1,0:T(8,128)(2,1)S(1)} collective-permute-done((bf16[2,4,128,128]{3,2,1,0:T(8,128)(2,1)S(1)}, bf16[2,4,128,128]{3,2,1,0:T(8,128)(2,1)S(1)}, u32[]{:S(2)}, u32[]{:S(2)}) %collective-permute-start.7) | collective-permute-done | bytes 262176 | tf_op jit(solution)/shard_map/ppermute | solution.py:26
  54.8 0.8 %kv_rows.1 = (bf16[128,4,128]{2,1,0:T(4,128)(2,1)}, bf16[128,4,128]{2,1,0:T(4,128)(2,1)}) custom-call(f32[2,4,128,128]{3,2,1,0:T(8,128)S(1)} %kv_sum.5.total_ref, bf16[2,4,128,128]{3,2,1,0:T(8,128)(2,1)S(1)} %collective-permute-done.7.part_ref), custom_call_target="tpu_custom_call" | custom-call | flops 131072 | bytes 1048576 | tf_op jit(solution)/shard_map/kv_rows/pallas_call | solution.py:214
  (1 shorter events, 0.0 us)
Async XLA Ops:
  1.7 17.7 %collective-permute-start.3 = (bf16[2,4,128,128]{3,2,1,0:T(8,128)(2,1)S(1)}, bf16[2,4,128,128]{3,2,1,0:T(8,128)(2,1)S(1)}, u32[]{:S(2)}, u32[]{:S(2)}) collective-permute-start(bf16[2,4,128,128]{3,2,1,0:T(8,128)(2,1)S(1)} %maximum_bitcast_fusion.kv_ref), channel_id=1, source_target_pairs={{0,192},{64,256},{128,320},{192,384},{256,448},{320,1},{384,65},{4... | collective-permute-start | bytes 786440 | tf_op jit(solution)/shard_map/ppermute | solution.py:26
  5.8 20.3 %collective-permute-start.2 = (bf16[2,4,128,128]{3,2,1,0:T(8,128)(2,1)S(1)}, bf16[2,4,128,128]{3,2,1,0:T(8,128)(2,1)S(1)}, u32[]{:S(2)}, u32[]{:S(2)}) collective-permute-start(bf16[2,4,128,128]{3,2,1,0:T(8,128)(2,1)S(1)} %maximum_bitcast_fusion.kv_ref), channel_id=1, source_target_pairs={{0,256},{64,320},{128,384},{192,448},{256,1},{320,65},{384,129},{4... | collective-permute-start | bytes 786440 | tf_op jit(solution)/shard_map/ppermute | solution.py:26
  10.2 24.7 %collective-permute-start.1 = (bf16[2,4,128,128]{3,2,1,0:T(8,128)(2,1)S(1)}, bf16[2,4,128,128]{3,2,1,0:T(8,128)(2,1)S(1)}, u32[]{:S(2)}, u32[]{:S(2)}) collective-permute-start(bf16[2,4,128,128]{3,2,1,0:T(8,128)(2,1)S(1)} %maximum_bitcast_fusion.kv_ref), channel_id=1, source_target_pairs={{0,128},{64,192},{128,256},{192,320},{256,384},{320,448},{384,1},{... | collective-permute-start | bytes 786440 | tf_op jit(solution)/shard_map/ppermute | solution.py:26
  14.3 29.0 %collective-permute-start = (bf16[2,4,128,128]{3,2,1,0:T(8,128)(2,1)S(1)}, bf16[2,4,128,128]{3,2,1,0:T(8,128)(2,1)S(1)}, u32[]{:S(2)}, u32[]{:S(2)}) collective-permute-start(bf16[2,4,128,128]{3,2,1,0:T(8,128)(2,1)S(1)} %maximum_bitcast_fusion.kv_ref), channel_id=1, source_target_pairs={{0,64},{64,128},{128,192},{192,256},{256,320},{320,384},{384,448},... | collective-permute-start | bytes 786440 | tf_op jit(solution)/shard_map/ppermute | solution.py:26
  16.4 1.8 %copy-start.3 = (bf16[128,32,128]{2,1,0:T(8,128)(2,1)S(1)}, bf16[128,32,128]{2,1,0:T(8,128)(2,1)}, u32[]{:S(2)}) copy-start(bf16[128,32,128]{2,1,0:T(8,128)(2,1)} %param.11) | copy-start | bytes 3145732
  16.4 2.2 %copy-start.4 = (s32[5]{0:T(128)S(1)}, s32[5]{0:T(128)}, u32[]{:S(2)}) copy-start(s32[5]{0:T(128)} %constant.23) | copy-start | bytes 64
  16.4 2.3 %copy-start = (f32[128,32]{0,1:T(8,128)S(1)}, f32[128,32]{0,1:T(8,128)}, u32[]{:S(2)}) copy-start(f32[128,32]{0,1:T(8,128)} %param.12) | copy-start | bytes 49156
  16.4 2.3 %copy-start.1 = (f32[128,32]{0,1:T(8,128)S(1)}, f32[128,32]{0,1:T(8,128)}, u32[]{:S(2)}) copy-start(f32[128,32]{0,1:T(8,128)} %param.13) | copy-start | bytes 49156
  16.4 2.3 %copy-start.2 = (s32[256]{0:T(256)S(1)}, s32[256]{0:T(256)}, u32[]{:S(2)}) copy-start(s32[256]{0:T(256)} %param.14) | copy-start | bytes 3076
  19.8 32.3 %collective-permute-start.4 = (bf16[2,4,128,128]{3,2,1,0:T(8,128)(2,1)S(1)}, bf16[2,4,128,128]{3,2,1,0:T(8,128)(2,1)S(1)}, u32[]{:S(2)}, u32[]{:S(2)}) collective-permute-start(bf16[2,4,128,128]{3,2,1,0:T(8,128)(2,1)S(1)} %get-tuple-element.27), channel_id=1, source_target_pairs={{192,0},{256,64},{320,128},{384,192},{448,256},{1,320},{65,384},{1... | collective-permute-start | bytes 786440 | tf_op jit(solution)/shard_map/ppermute | solution.py:26
  26.7 25.5 %collective-permute-start.5 = (bf16[2,4,128,128]{3,2,1,0:T(8,128)(2,1)S(1)}, bf16[2,4,128,128]{3,2,1,0:T(8,128)(2,1)S(1)}, u32[]{:S(2)}, u32[]{:S(2)}) collective-permute-start(bf16[2,4,128,128]{3,2,1,0:T(8,128)(2,1)S(1)} %get-tuple-element.28), channel_id=1, source_target_pairs={{256,0},{320,64},{384,128},{448,192},{1,256},{65,320},{129,384},{1... | collective-permute-start | bytes 786440 | tf_op jit(solution)/shard_map/ppermute | solution.py:26
  35.4 17.0 %collective-permute-start.6 = (bf16[2,4,128,128]{3,2,1,0:T(8,128)(2,1)S(1)}, bf16[2,4,128,128]{3,2,1,0:T(8,128)(2,1)S(1)}, u32[]{:S(2)}, u32[]{:S(2)}) collective-permute-start(bf16[2,4,128,128]{3,2,1,0:T(8,128)(2,1)S(1)} %get-tuple-element.29), channel_id=1, source_target_pairs={{128,0},{192,64},{256,128},{320,192},{384,256},{448,320},{1,384},{... | collective-permute-start | bytes 786440 | tf_op jit(solution)/shard_map/ppermute | solution.py:26
  45.4 9.3 %collective-permute-start.7 = (bf16[2,4,128,128]{3,2,1,0:T(8,128)(2,1)S(1)}, bf16[2,4,128,128]{3,2,1,0:T(8,128)(2,1)S(1)}, u32[]{:S(2)}, u32[]{:S(2)}) collective-permute-start(bf16[2,4,128,128]{3,2,1,0:T(8,128)(2,1)S(1)} %get-tuple-element.30), channel_id=1, source_target_pairs={{64,0},{128,64},{192,128},{256,192},{320,256},{384,320},{448,384},... | collective-permute-start | bytes 786440 | tf_op jit(solution)/shard_map/ppermute | solution.py:26

commit v4 on v3

--- a/solution.py
+++ b/solution.py
@@ -87,44 +87,29 @@
     query_total_ref, kv_part_ref = rest[-2:]
     groups, cols, _ = query_ref.shape
     rows = kv_ref.shape[2]
-    def work():
-        key_pos = lax.broadcasted_iota(jnp.int32, (rows, cols), 0)
-        allowed = key_pos >= start_ref[slot]
-        if slot == 0:
-            query_pos = lax.broadcasted_iota(jnp.int32, (rows, cols), 1) & (rows - 1)
-            allowed = allowed & (key_pos <= query_pos)
-        for group in range(groups):
-            keys = kv_ref[0, group]
-            values = kv_ref[1, group]
-            query_rows = query_ref[group]
-            grad_rows = grad_ref[group]
-            scores = contract(keys, query_rows, (1, 1))
-            prob_grad = contract(values, grad_rows, (1, 1))
-            prob = jnp.exp2(scores * (softmax_scale * LOG2E) - norm_ref[group])
-            prob = jnp.where(allowed, prob, 0.0)
-            score_grad = (prob * (prob_grad - delta_ref[group])).astype(jnp.bfloat16)
-            value_part = contract(prob.astype(jnp.bfloat16), grad_rows, (1, 0))
-            key_part = contract(score_grad, query_rows, (1, 0)) * softmax_scale
-            query_part = contract(keys, score_grad, (0, 0))
-            if query_in_ref is not None:
-                query_part += query_in_ref[group]
-            query_total_ref[group] = query_part
-            kv_part_ref[0, group] = key_part.astype(kv_part_ref.dtype)
-            kv_part_ref[1, group] = value_part.astype(kv_part_ref.dtype)
-
+    key_pos = lax.broadcasted_iota(jnp.int32, (rows, cols), 0)
+    allowed = key_pos >= start_ref[slot]
     if slot == 0:
-        work()
-        return
-    needed = jnp.min(start_ref[slot, :, pl.ds(0, rows)]) < rows
-    pl.when(needed)(work)
-
-    @pl.when(jnp.logical_not(needed))
-    def _():
-        if query_in_ref is None:
-            query_total_ref[...] = jnp.zeros_like(query_total_ref)
-        else:
-            query_total_ref[...] = query_in_ref[...]
-        kv_part_ref[...] = jnp.zeros_like(kv_part_ref)
+        query_pos = lax.broadcasted_iota(jnp.int32, (rows, cols), 1) & (rows - 1)
+        allowed = allowed & (key_pos <= query_pos)
+    for group in range(groups):
+        keys = kv_ref[0, group]
+        values = kv_ref[1, group]
+        query_rows = query_ref[group]
+        grad_rows = grad_ref[group]
+        scores = contract(keys, query_rows, (1, 1))
+        prob_grad = contract(values, grad_rows, (1, 1))
+        prob = jnp.exp2(scores * (softmax_scale * LOG2E) - norm_ref[group])
+        prob = jnp.where(allowed, prob, 0.0)
+        score_grad = (prob * (prob_grad - delta_ref[group])).astype(jnp.bfloat16)
+        value_part = contract(prob.astype(jnp.bfloat16), grad_rows, (1, 0))
+        key_part = contract(score_grad, query_rows, (1, 0)) * softmax_scale
+        query_part = contract(keys, score_grad, (0, 0))
+        if query_in_ref is not None:
+            query_part += query_in_ref[group]
+        query_total_ref[group] = query_part
+        kv_part_ref[0, group] = key_part.astype(kv_part_ref.dtype)
+        kv_part_ref[1, group] = value_part.astype(kv_part_ref.dtype)
 
 
 def tile_call(slot, starts, norms, deltas, queries, grads, kv, query_total=None):

time: 55.9 us -> 55.8 us (level)
  the two profiles are of different devices: /device:TPU:321 before, /device:TPU:17 now
where the time goes in v4:
time: 55.8 us; the launch traced here: 55.5 us
  starting transfers between devices  28.9 us (52%)
  Pallas kernels  12.2 us (22%)
  waiting for transfers between devices  8.53 us (15%)
  local copies, waits for them, and re-layouts  4.81 us (9%)
  between operations  0.9 us (2%)
    ppermute x8, starting transfers between devices, chunk_permute(): return lax.ppermute(x, ('head', 'ctx'), pairs)  28.9 us
    pallas_call x5, Pallas kernels, tile_call(): pl.pallas_call(functools.partial(tile_kernel, slot, 1.0 / math.sqrt(dim))...  9.61 us
    ppermute x8, waiting for transfers between devices, chunk_permute(): return lax.ppermute(x, ('head', 'ctx'), pairs)  8.53 us
    transpose x2, local copies, waits for them, and re-layouts, shards(): jnp.transpose(x, (1, 0, 2)).reshape(KV_HEADS, group * rows, dim)  2.12 us
    reshape x1, local copies, waits for them, and re-layouts, shards(): query_grad = jnp.transpose(query_heads.reshape(heads, rows, dim), (1, 0, 2))  1.65 us
  transfers between devices with their start and end apart: 8, of which 2 were waited for; matrix products, arithmetic and copies ran while one was open for 7% of the time, Pallas kernels for 21%

profile of v4, /device:TPU:17, one launch (start us, length us, event | category | flops | bytes accessed | tf_op | source)
XLA Modules:
  0.0 55.5 jit_solution(15210817767123612555)
XLA Ops:
  0.6 1.0 %copy_bitcast_fusion.1 = (bf16[1,128,4,128]{3,1,2,0:T(8,128)(2,1)S(1)}, bf16[1,128,4,128]{3,1,2,0:T(8,128)(2,1)S(1)}) fusion(bf16[128,4,128]{2,1,0:T(4,128)(2,1)} %param.10, bf16[128,4,128]{2,1,0:T(4,128)(2,1)} %param.9), kind=kLoop, calls=%fused_computation.2 | loop fusion | bytes 524288 | tf_op jit(solution)/shard_map/stack | solution.py:218
  1.7 4.1 %collective-permute-start.3 = (bf16[2,4,128,128]{3,2,1,0:T(8,128)(2,1)S(1)}, bf16[2,4,128,128]{3,2,1,0:T(8,128)(2,1)S(1)}, u32[]{:S(2)}, u32[]{:S(2)}) collective-permute-start(bf16[2,4,128,128]{3,2,1,0:T(8,128)(2,1)S(1)} %maximum_bitcast_fusion.kv_ref), channel_id=1, source_target_pairs={{0,192},{64,256},{128,320},{192,384},{256,448},{320,1},{384,65},{4... | collective-permute-start | bytes 786440 | tf_op jit(solution)/shard_map/ppermute | solution.py:26
  5.8 4.4 %collective-permute-start.2 = (bf16[2,4,128,128]{3,2,1,0:T(8,128)(2,1)S(1)}, bf16[2,4,128,128]{3,2,1,0:T(8,128)(2,1)S(1)}, u32[]{:S(2)}, u32[]{:S(2)}) collective-permute-start(bf16[2,4,128,128]{3,2,1,0:T(8,128)(2,1)S(1)} %maximum_bitcast_fusion.kv_ref), channel_id=1, source_target_pairs={{0,256},{64,320},{128,384},{192,448},{256,1},{320,65},{384,129},{4... | collective-permute-start | bytes 786440 | tf_op jit(solution)/shard_map/ppermute | solution.py:26
  10.2 4.4 %collective-permute-start.1 = (bf16[2,4,128,128]{3,2,1,0:T(8,128)(2,1)S(1)}, bf16[2,4,128,128]{3,2,1,0:T(8,128)(2,1)S(1)}, u32[]{:S(2)}, u32[]{:S(2)}) collective-permute-start(bf16[2,4,128,128]{3,2,1,0:T(8,128)(2,1)S(1)} %maximum_bitcast_fusion.kv_ref), channel_id=1, source_target_pairs={{0,128},{64,192},{128,256},{192,320},{256,384},{320,448},{384,1},{... | collective-permute-start | bytes 786440 | tf_op jit(solution)/shard_map/ppermute | solution.py:26
  14.6 3.0 %collective-permute-start = (bf16[2,4,128,128]{3,2,1,0:T(8,128)(2,1)S(1)}, bf16[2,4,128,128]{3,2,1,0:T(8,128)(2,1)S(1)}, u32[]{:S(2)}, u32[]{:S(2)}) collective-permute-start(bf16[2,4,128,128]{3,2,1,0:T(8,128)(2,1)S(1)} %maximum_bitcast_fusion.kv_ref), channel_id=1, source_target_pairs={{0,64},{64,128},{128,192},{192,256},{256,320},{320,384},{384,448},... | collective-permute-start | bytes 786440 | tf_op jit(solution)/shard_map/ppermute | solution.py:26
  17.6 0.0 copy-start.3
  17.6 0.0 copy-start.4
  17.6 0.0 copy-start
  17.6 0.0 copy-start.1
  17.7 0.0 copy-start.2
  17.7 1.7 %copy.18 = bf16[32,128,128]{2,1,0:T(8,128)(2,1)S(1)} copy(bf16[32,128,128]{2,0,1:T(8,128)(2,1)} %bitcast.32) | data formatting | bytes 2097152 | tf_op jit(solution)/shard_map/transpose | solution.py:221
  19.4 0.0 copy-done.3
  19.4 0.4 copy.19
  19.8 0.0 copy-done.4
  19.8 0.1 pad_add_fusion.place_ref
  19.9 0.0 copy-done
  19.9 0.0 copy-done.1
  19.9 0.0 copy-done.2
  19.9 0.7 %row_terms.1 = (s32[5,1,1024]{2,1,0:T(1,128)S(1)}, f32[4,1,1024]{2,1,0:T(1,128)S(1)}, f32[4,1,1024]{2,1,0:T(1,128)S(1)}) custom-call(s32[6]{0:T(128)S(1)} %pad_add_fusion.place_ref, f32[32,128]{1,0:T(8,128)S(1)} %bitcast.29, f32[32,128]{1,0:T(8,128)S(1)} %bitcast.30, s32[1,256]{1,0:T(1,128)S(1)} %bitcast.31), custom_call_target="tpu_custom_call" | custom-call | tf_op jit(solution)/shard_map/row_terms/pallas_call | solution.py:65
  20.6 0.0 collective-permute-done.3.kv_ref
  20.6 1.7 %tiles_1.1 = (f32[4,128,1024]{2,1,0:T(8,128)S(1)}, bf16[2,4,128,128]{3,2,1,0:T(8,128)(2,1)S(1)}) custom-call(s32[5,1,1024]{2,1,0:T(1,128)S(1)} %get-tuple-element.18.start_ref, f32[4,1,1024]{2,1,0:T(1,128)S(1)} %get-tuple-element.19.norm_ref, f32[4,1,1024]{2,1,0:T(1,128)S(1)} %get-tuple-element.20.delta_ref, bf16[4,1024,128]{2,1,0:T(8,128)(2,1)S(1)} %bitcast.18, ...), custom_call_target="tpu_custom_call" | custom-call | flops 671088640 | bytes 3145728 | tf_op jit(solution)/shard_map/tiles_1/pallas_call | solution.py:124
  22.3 3.6 %collective-permute-start.4 = (bf16[2,4,128,128]{3,2,1,0:T(8,128)(2,1)S(1)}, bf16[2,4,128,128]{3,2,1,0:T(8,128)(2,1)S(1)}, u32[]{:S(2)}, u32[]{:S(2)}) collective-permute-start(bf16[2,4,128,128]{3,2,1,0:T(8,128)(2,1)S(1)} %get-tuple-element.27), channel_id=1, source_target_pairs={{192,0},{256,64},{320,128},{384,192},{448,256},{1,320},{65,384},{1... | collective-permute-start | bytes 786440 | tf_op jit(solution)/shard_map/ppermute | solution.py:26
  25.9 1.8 %collective-permute-done.2.kv_ref = bf16[2,4,128,128]{3,2,1,0:T(8,128)(2,1)S(1)} collective-permute-done((bf16[2,4,128,128]{3,2,1,0:T(8,128)(2,1)S(1)}, bf16[2,4,128,128]{3,2,1,0:T(8,128)(2,1)S(1)}, u32[]{:S(2)}, u32[]{:S(2)}) %collective-permute-start.2) | collective-permute-done | bytes 262176 | tf_op jit(solution)/shard_map/ppermute | solution.py:26
  27.8 2.0 %tiles_2.1 = (f32[4,128,1024]{2,1,0:T(8,128)S(1)}, bf16[2,4,128,128]{3,2,1,0:T(8,128)(2,1)S(1)}) custom-call(s32[5,1,1024]{2,1,0:T(1,128)S(1)} %get-tuple-element.18.start_ref, f32[4,1,1024]{2,1,0:T(1,128)S(1)} %get-tuple-element.19.norm_ref, f32[4,1,1024]{2,1,0:T(1,128)S(1)} %get-tuple-element.20.delta_ref, ...), custom_call_target="tpu_custom_call", output_to_operand_aliasing={{0}: (6, {})} | custom-call | flops 671088640 | bytes 3145728 | tf_op jit(solution)/shard_map/tiles_2/pallas_call | solution.py:124
  29.7 3.3 %collective-permute-start.5 = (bf16[2,4,128,128]{3,2,1,0:T(8,128)(2,1)S(1)}, bf16[2,4,128,128]{3,2,1,0:T(8,128)(2,1)S(1)}, u32[]{:S(2)}, u32[]{:S(2)}) collective-permute-start(bf16[2,4,128,128]{3,2,1,0:T(8,128)(2,1)S(1)} %get-tuple-element.28), channel_id=1, source_target_pairs={{256,0},{320,64},{384,128},{448,192},{1,256},{65,320},{129,384},{1... | collective-permute-start | bytes 786440 | tf_op jit(solution)/shard_map/ppermute | solution.py:26
  33.0 0.0 collective-permute-done.1.kv_ref
  33.1 2.0 %tiles_3.1 = (f32[4,128,1024]{2,1,0:T(8,128)S(1)}, bf16[2,4,128,128]{3,2,1,0:T(8,128)(2,1)S(1)}) custom-call(s32[5,1,1024]{2,1,0:T(1,128)S(1)} %get-tuple-element.18.start_ref, f32[4,1,1024]{2,1,0:T(1,128)S(1)} %get-tuple-element.19.norm_ref, f32[4,1,1024]{2,1,0:T(1,128)S(1)} %get-tuple-element.20.delta_ref, ...), custom_call_target="tpu_custom_call", output_to_operand_aliasing={{0}: (6, {})} | custom-call | flops 671088640 | bytes 3145728 | tf_op jit(solution)/shard_map/tiles_3/pallas_call | solution.py:124
  35.0 3.7 %collective-permute-start.6 = (bf16[2,4,128,128]{3,2,1,0:T(8,128)(2,1)S(1)}, bf16[2,4,128,128]{3,2,1,0:T(8,128)(2,1)S(1)}, u32[]{:S(2)}, u32[]{:S(2)}) collective-permute-start(bf16[2,4,128,128]{3,2,1,0:T(8,128)(2,1)S(1)} %get-tuple-element.29), channel_id=1, source_target_pairs={{128,0},{192,64},{256,128},{320,192},{384,256},{448,320},{1,384},{... | collective-permute-start | bytes 786440 | tf_op jit(solution)/shard_map/ppermute | solution.py:26
  38.7 0.0 collective-permute-done.kv_ref
  38.7 2.0 %tiles_4.1 = (f32[4,128,1024]{2,1,0:T(8,128)S(1)}, bf16[2,4,128,128]{3,2,1,0:T(8,128)(2,1)S(1)}) custom-call(s32[5,1,1024]{2,1,0:T(1,128)S(1)} %get-tuple-element.18.start_ref, f32[4,1,1024]{2,1,0:T(1,128)S(1)} %get-tuple-element.19.norm_ref, f32[4,1,1024]{2,1,0:T(1,128)S(1)} %get-tuple-element.20.delta_ref, ...), custom_call_target="tpu_custom_call", output_to_operand_aliasing={{0}: (6, {})} | custom-call | flops 671088640 | bytes 3145728 | tf_op jit(solution)/shard_map/tiles_4/pallas_call | solution.py:124
  40.7 2.4 %collective-permute-start.7 = (bf16[2,4,128,128]{3,2,1,0:T(8,128)(2,1)S(1)}, bf16[2,4,128,128]{3,2,1,0:T(8,128)(2,1)S(1)}, u32[]{:S(2)}, u32[]{:S(2)}) collective-permute-start(bf16[2,4,128,128]{3,2,1,0:T(8,128)(2,1)S(1)} %get-tuple-element.30), channel_id=1, source_target_pairs={{64,0},{128,64},{192,128},{256,192},{320,256},{384,320},{448,384},... | collective-permute-start | bytes 786440 | tf_op jit(solution)/shard_map/ppermute | solution.py:26
  43.1 2.1 %tiles_0.1 = (f32[4,128,1024]{2,1,0:T(8,128)S(1)}, f32[2,4,128,128]{3,2,1,0:T(8,128)S(1)}) custom-call(s32[5,1,1024]{2,1,0:T(1,128)S(1)} %get-tuple-element.18.start_ref, f32[4,1,1024]{2,1,0:T(1,128)S(1)} %get-tuple-element.19.norm_ref, f32[4,1,1024]{2,1,0:T(1,128)S(1)} %get-tuple-element.20.delta_ref, ...), custom_call_target="tpu_custom_call", output_to_operand_aliasing={{0}: (6, {})} | custom-call | flops 671088640 | bytes 3145728 | tf_op jit(solution)/shard_map/tiles_0/pallas_call | solution.py:124
  45.1 0.8 %query_rows.1 = bf16[4,8,128,128]{3,2,1,0:T(8,128)(2,1)S(1)} custom-call(f32[4,128,1024]{2,1,0:T(8,128)S(1)} %get-tuple-element.25.total_ref), custom_call_target="tpu_custom_call" | custom-call | flops 524288 | bytes 3145728 | tf_op jit(solution)/shard_map/query_rows/pallas_call | solution.py:158
  46.0 1.6 %copy.26 = bf16[32,128,128]{2,0,1:T(8,128)(2,1)} copy(bf16[32,128,128]{2,1,0:T(8,128)(2,1)S(1)} %bitcast.28) | data formatting | bytes 2097152 | tf_op jit(solution)/shard_map/reshape | solution.py:238
  47.6 0.0 collective-permute-done.4.part_ref
  47.6 0.1 kv_sum.3.total_ref
  47.7 0.0 collective-permute-done.5.part_ref
  47.7 0.1 kv_sum.4.total_ref
  47.8 0.0 collective-permute-done.6.part_ref
  47.8 0.1 kv_sum.5.total_ref
  48.0 6.7 %collective-permute-done.7.part_ref = bf16[2,4,128,128]{3,2,1,0:T(8,128)(2,1)S(1)} collective-permute-done((bf16[2,4,128,128]{3,2,1,0:T(8,128)(2,1)S(1)}, bf16[2,4,128,128]{3,2,1,0:T(8,128)(2,1)S(1)}, u32[]{:S(2)}, u32[]{:S(2)}) %collective-permute-start.7) | collective-permute-done | bytes 262176 | tf_op jit(solution)/shard_map/ppermute | solution.py:26
  54.7 0.8 %kv_rows.1 = (bf16[128,4,128]{2,1,0:T(4,128)(2,1)}, bf16[128,4,128]{2,1,0:T(4,128)(2,1)}) custom-call(f32[2,4,128,128]{3,2,1,0:T(8,128)S(1)} %kv_sum.5.total_ref, bf16[2,4,128,128]{3,2,1,0:T(8,128)(2,1)S(1)} %collective-permute-done.7.part_ref), custom_call_target="tpu_custom_call" | custom-call | flops 131072 | bytes 1048576 | tf_op jit(solution)/shard_map/kv_rows/pallas_call | solution.py:199
  (1 shorter events, 0.0 us)
Async XLA Ops:
  1.7 18.9 %collective-permute-start.3 = (bf16[2,4,128,128]{3,2,1,0:T(8,128)(2,1)S(1)}, bf16[2,4,128,128]{3,2,1,0:T(8,128)(2,1)S(1)}, u32[]{:S(2)}, u32[]{:S(2)}) collective-permute-start(bf16[2,4,128,128]{3,2,1,0:T(8,128)(2,1)S(1)} %maximum_bitcast_fusion.kv_ref), channel_id=1, source_target_pairs={{0,192},{64,256},{128,320},{192,384},{256,448},{320,1},{384,65},{4... | collective-permute-start | bytes 786440 | tf_op jit(solution)/shard_map/ppermute | solution.py:26
  5.8 21.9 %collective-permute-start.2 = (bf16[2,4,128,128]{3,2,1,0:T(8,128)(2,1)S(1)}, bf16[2,4,128,128]{3,2,1,0:T(8,128)(2,1)S(1)}, u32[]{:S(2)}, u32[]{:S(2)}) collective-permute-start(bf16[2,4,128,128]{3,2,1,0:T(8,128)(2,1)S(1)} %maximum_bitcast_fusion.kv_ref), channel_id=1, source_target_pairs={{0,256},{64,320},{128,384},{192,448},{256,1},{320,65},{384,129},{4... | collective-permute-start | bytes 786440 | tf_op jit(solution)/shard_map/ppermute | solution.py:26
  10.2 22.9 %collective-permute-start.1 = (bf16[2,4,128,128]{3,2,1,0:T(8,128)(2,1)S(1)}, bf16[2,4,128,128]{3,2,1,0:T(8,128)(2,1)S(1)}, u32[]{:S(2)}, u32[]{:S(2)}) collective-permute-start(bf16[2,4,128,128]{3,2,1,0:T(8,128)(2,1)S(1)} %maximum_bitcast_fusion.kv_ref), channel_id=1, source_target_pairs={{0,128},{64,192},{128,256},{192,320},{256,384},{320,448},{384,1},{... | collective-permute-start | bytes 786440 | tf_op jit(solution)/shard_map/ppermute | solution.py:26
  14.6 24.1 %collective-permute-start = (bf16[2,4,128,128]{3,2,1,0:T(8,128)(2,1)S(1)}, bf16[2,4,128,128]{3,2,1,0:T(8,128)(2,1)S(1)}, u32[]{:S(2)}, u32[]{:S(2)}) collective-permute-start(bf16[2,4,128,128]{3,2,1,0:T(8,128)(2,1)S(1)} %maximum_bitcast_fusion.kv_ref), channel_id=1, source_target_pairs={{0,64},{64,128},{128,192},{192,256},{256,320},{320,384},{384,448},... | collective-permute-start | bytes 786440 | tf_op jit(solution)/shard_map/ppermute | solution.py:26
  17.6 1.8 %copy-start.3 = (bf16[128,32,128]{2,1,0:T(8,128)(2,1)S(1)}, bf16[128,32,128]{2,1,0:T(8,128)(2,1)}, u32[]{:S(2)}) copy-start(bf16[128,32,128]{2,1,0:T(8,128)(2,1)} %param.11) | copy-start | bytes 3145732
  17.6 2.2 %copy-start.4 = (s32[5]{0:T(128)S(1)}, s32[5]{0:T(128)}, u32[]{:S(2)}) copy-start(s32[5]{0:T(128)} %constant.23) | copy-start | bytes 64
  17.6 2.3 %copy-start = (f32[128,32]{0,1:T(8,128)S(1)}, f32[128,32]{0,1:T(8,128)}, u32[]{:S(2)}) copy-start(f32[128,32]{0,1:T(8,128)} %param.12) | copy-start | bytes 49156
  17.6 2.3 %copy-start.1 = (f32[128,32]{0,1:T(8,128)S(1)}, f32[128,32]{0,1:T(8,128)}, u32[]{:S(2)}) copy-start(f32[128,32]{0,1:T(8,128)} %param.13) | copy-start | bytes 49156
  17.7 2.3 %copy-start.2 = (s32[256]{0:T(256)S(1)}, s32[256]{0:T(256)}, u32[]{:S(2)}) copy-start(s32[256]{0:T(256)} %param.14) | copy-start | bytes 3076
  22.3 25.3 %collective-permute-start.4 = (bf16[2,4,128,128]{3,2,1,0:T(8,128)(2,1)S(1)}, bf16[2,4,128,128]{3,2,1,0:T(8,128)(2,1)S(1)}, u32[]{:S(2)}, u32[]{:S(2)}) collective-permute-start(bf16[2,4,128,128]{3,2,1,0:T(8,128)(2,1)S(1)} %get-tuple-element.27), channel_id=1, source_target_pairs={{192,0},{256,64},{320,128},{384,192},{448,256},{1,320},{65,384},{1... | collective-permute-start | bytes 786440 | tf_op jit(solution)/shard_map/ppermute | solution.py:26
  29.7 18.0 %collective-permute-start.5 = (bf16[2,4,128,128]{3,2,1,0:T(8,128)(2,1)S(1)}, bf16[2,4,128,128]{3,2,1,0:T(8,128)(2,1)S(1)}, u32[]{:S(2)}, u32[]{:S(2)}) collective-permute-start(bf16[2,4,128,128]{3,2,1,0:T(8,128)(2,1)S(1)} %get-tuple-element.28), channel_id=1, source_target_pairs={{256,0},{320,64},{384,128},{448,192},{1,256},{65,320},{129,384},{1... | collective-permute-start | bytes 786440 | tf_op jit(solution)/shard_map/ppermute | solution.py:26
  35.0 12.8 %collective-permute-start.6 = (bf16[2,4,128,128]{3,2,1,0:T(8,128)(2,1)S(1)}, bf16[2,4,128,128]{3,2,1,0:T(8,128)(2,1)S(1)}, u32[]{:S(2)}, u32[]{:S(2)}) collective-permute-start(bf16[2,4,128,128]{3,2,1,0:T(8,128)(2,1)S(1)} %get-tuple-element.29), channel_id=1, source_target_pairs={{128,0},{192,64},{256,128},{320,192},{384,256},{448,320},{1,384},{... | collective-permute-start | bytes 786440 | tf_op jit(solution)/shard_map/ppermute | solution.py:26
  40.7 14.0 %collective-permute-start.7 = (bf16[2,4,128,128]{3,2,1,0:T(8,128)(2,1)S(1)}, bf16[2,4,128,128]{3,2,1,0:T(8,128)(2,1)S(1)}, u32[]{:S(2)}, u32[]{:S(2)}) collective-permute-start(bf16[2,4,128,128]{3,2,1,0:T(8,128)(2,1)S(1)} %get-tuple-element.30), channel_id=1, source_target_pairs={{64,0},{128,64},{192,128},{256,192},{320,256},{384,320},{448,384},... | collective-permute-start | bytes 786440 | tf_op jit(solution)/shard_map/ppermute | solution.py:26

commit v5 on v4

--- a/solution.py
+++ b/solution.py
@@ -30,6 +30,23 @@
     return lax.dot_general(
         left, right, ((dims[:1], dims[1:]), ((), ())), preferred_element_type=jnp.float32
     )
+
+
+def stack_kernel(key_ref, value_ref, out_ref):
+    out_ref[0] = key_ref[...]
+    out_ref[1] = value_ref[...]
+
+
+def stack_call(keys, values):
+    whole = pl.BlockSpec(memory_space=pltpu.VMEM)
+    return pl.pallas_call(
+        stack_kernel,
+        in_specs=[whole, whole],
+        out_specs=whole,
+        out_shape=jax.ShapeDtypeStruct((2, *keys.shape), keys.dtype),
+        compiler_params=pltpu.CompilerParams(vmem_limit_bytes=VMEM_LIMIT),
+        name="kv_stack",
+    )(keys, values)
 
 
 def rows_kernel(place_ref, norm_ref, delta_ref, length_ref, start_ref, norm_out, delta_out):
@@ -215,7 +232,7 @@
     chunk = lax.axis_index("ctx") * lax.axis_size("head") + lax.axis_index("head")
     first_pos = chunk * rows
 
-    kv = jnp.transpose(jnp.stack([key_states, value_states]), (0, 2, 1, 3))
+    kv = stack_call(jnp.transpose(key_states, (1, 0, 2)), jnp.transpose(value_states, (1, 0, 2)))
     behind = {distance: chunk_permute(kv, lambda c, d=distance: c + d) for distance in ORDER}
 
     by_head = lambda x: jnp.transpose(x, (1, 0, 2)).reshape(KV_HEADS, group * rows, dim)

time: 55.8 us -> 55.8 us (level)
  the two profiles are of different devices: /device:TPU:17 before, /device:TPU:449 now
where the time goes in v5:
time: 55.8 us; the launch traced here: 55.5 us
  starting transfers between devices  35.9 us (64%)
  Pallas kernels  12.3 us (22%)
  local copies, waits for them, and re-layouts  4.81 us (9%)
  waiting for transfers between devices  1.52 us (3%)
  between operations  0.9 us (2%)
    ppermute x8, starting transfers between devices, chunk_permute(): return lax.ppermute(x, ('head', 'ctx'), pairs)  35.9 us
    pallas_call x5, Pallas kernels, tile_call(): pl.pallas_call(functools.partial(tile_kernel, slot, 1.0 / math.sqrt(dim))...  9.63 us
    transpose x2, local copies, waits for them, and re-layouts, shards(): jnp.transpose(x, (1, 0, 2)).reshape(KV_HEADS, group * rows, dim)  2.12 us
    reshape x1, local copies, waits for them, and re-layouts, shards(): query_grad = jnp.transpose(query_heads.reshape(heads, rows, dim), (1, 0, 2))  1.65 us
    ppermute x8, waiting for transfers between devices, chunk_permute(): return lax.ppermute(x, ('head', 'ctx'), pairs)  1.52 us
  transfers between devices with their start and end apart: 8, of which 1 were waited for; matrix products, arithmetic and copies ran while one was open for 7% of the time, Pallas kernels for 21%

profile of v5, /device:TPU:449, one launch (start us, length us, event | category | flops | bytes accessed | tf_op | source)
XLA Modules:
  0.0 55.5 jit_solution(16861928457970979498)
XLA Ops:
  0.6 1.0 %copy_bitcast_fusion.1 = (bf16[4,128,128]{2,1,0:T(8,128)(2,1)S(1)}, bf16[4,128,128]{2,1,0:T(8,128)(2,1)S(1)}) fusion(bf16[128,4,128]{2,1,0:T(4,128)(2,1)} %param.10, bf16[128,4,128]{2,1,0:T(4,128)(2,1)} %param.9), kind=kLoop, calls=%fused_computation.1 | loop fusion | bytes 524288 | tf_op jit(solution)/shard_map/transpose | solution.py:235
  1.7 4.1 %collective-permute-start.3 = (bf16[2,4,128,128]{3,2,1,0:T(8,128)(2,1)S(1)}, bf16[2,4,128,128]{3,2,1,0:T(8,128)(2,1)S(1)}, u32[]{:S(2)}, u32[]{:S(2)}) collective-permute-start(bf16[2,4,128,128]{3,2,1,0:T(8,128)(2,1)S(1)} %kv_stack.1.kv_ref), channel_id=1, source_target_pairs={{0,192},{64,256},{128,320},{192,384},{256,448},{320,1},{384,65},{4... | collective-permute-start | bytes 786440 | tf_op jit(solution)/shard_map/ppermute | solution.py:26
  5.8 4.4 %collective-permute-start.2 = (bf16[2,4,128,128]{3,2,1,0:T(8,128)(2,1)S(1)}, bf16[2,4,128,128]{3,2,1,0:T(8,128)(2,1)S(1)}, u32[]{:S(2)}, u32[]{:S(2)}) collective-permute-start(bf16[2,4,128,128]{3,2,1,0:T(8,128)(2,1)S(1)} %kv_stack.1.kv_ref), channel_id=1, source_target_pairs={{0,256},{64,320},{128,384},{192,448},{256,1},{320,65},{384,129},{4... | collective-permute-start | bytes 786440 | tf_op jit(solution)/shard_map/ppermute | solution.py:26
  10.2 4.1 %collective-permute-start.1 = (bf16[2,4,128,128]{3,2,1,0:T(8,128)(2,1)S(1)}, bf16[2,4,128,128]{3,2,1,0:T(8,128)(2,1)S(1)}, u32[]{:S(2)}, u32[]{:S(2)}) collective-permute-start(bf16[2,4,128,128]{3,2,1,0:T(8,128)(2,1)S(1)} %kv_stack.1.kv_ref), channel_id=1, source_target_pairs={{0,128},{64,192},{128,256},{192,320},{256,384},{320,448},{384,1},{... | collective-permute-start | bytes 786440 | tf_op jit(solution)/shard_map/ppermute | solution.py:26
  14.3 2.1 %collective-permute-start = (bf16[2,4,128,128]{3,2,1,0:T(8,128)(2,1)S(1)}, bf16[2,4,128,128]{3,2,1,0:T(8,128)(2,1)S(1)}, u32[]{:S(2)}, u32[]{:S(2)}) collective-permute-start(bf16[2,4,128,128]{3,2,1,0:T(8,128)(2,1)S(1)} %kv_stack.1.kv_ref), channel_id=1, source_target_pairs={{0,64},{64,128},{128,192},{192,256},{256,320},{320,384},{384,448},... | collective-permute-start | bytes 786440 | tf_op jit(solution)/shard_map/ppermute | solution.py:26
  16.4 0.0 copy-start.3
  16.4 0.0 copy-start.4
  16.4 0.0 copy-start
  16.4 0.0 copy-start.1
  16.4 0.0 copy-start.2
  16.4 1.7 %copy.18 = bf16[32,128,128]{2,1,0:T(8,128)(2,1)S(1)} copy(bf16[32,128,128]{2,0,1:T(8,128)(2,1)} %bitcast.30) | data formatting | bytes 2097152 | tf_op jit(solution)/shard_map/transpose | solution.py:238
  18.2 0.0 copy-done.3
  18.2 0.4 copy.19
  18.6 0.0 copy-done.4
  18.6 0.1 pad_add_fusion.place_ref
  18.7 0.0 copy-done
  18.7 0.0 copy-done.1
  18.7 0.0 copy-done.2
  18.7 0.7 %row_terms.1 = (s32[5,1,1024]{2,1,0:T(1,128)S(1)}, f32[4,1,1024]{2,1,0:T(1,128)S(1)}, f32[4,1,1024]{2,1,0:T(1,128)S(1)}) custom-call(s32[6]{0:T(128)S(1)} %pad_add_fusion.place_ref, f32[32,128]{1,0:T(8,128)S(1)} %bitcast.27, f32[32,128]{1,0:T(8,128)S(1)} %bitcast.28, s32[1,256]{1,0:T(1,128)S(1)} %bitcast.29), custom_call_target="tpu_custom_call" | custom-call | tf_op jit(solution)/shard_map/row_terms/pallas_call | solution.py:82
  19.4 0.0 collective-permute-done.3.kv_ref
  19.4 1.7 %tiles_1.1 = (f32[4,128,1024]{2,1,0:T(8,128)S(1)}, bf16[2,4,128,128]{3,2,1,0:T(8,128)(2,1)S(1)}) custom-call(s32[5,1,1024]{2,1,0:T(1,128)S(1)} %get-tuple-element.18.start_ref, f32[4,1,1024]{2,1,0:T(1,128)S(1)} %get-tuple-element.19.norm_ref, f32[4,1,1024]{2,1,0:T(1,128)S(1)} %get-tuple-element.20.delta_ref, bf16[4,1024,128]{2,1,0:T(8,128)(2,1)S(1)} %bitcast.16, ...), custom_call_target="tpu_custom_call" | custom-call | flops 671088640 | bytes 3145728 | tf_op jit(solution)/shard_map/tiles_1/pallas_call | solution.py:141
  21.1 4.8 %collective-permute-start.4 = (bf16[2,4,128,128]{3,2,1,0:T(8,128)(2,1)S(1)}, bf16[2,4,128,128]{3,2,1,0:T(8,128)(2,1)S(1)}, u32[]{:S(2)}, u32[]{:S(2)}) collective-permute-start(bf16[2,4,128,128]{3,2,1,0:T(8,128)(2,1)S(1)} %get-tuple-element.27), channel_id=1, source_target_pairs={{192,0},{256,64},{320,128},{384,192},{448,256},{1,320},{65,384},{1... | collective-permute-start | bytes 786440 | tf_op jit(solution)/shard_map/ppermute | solution.py:26
  25.9 0.0 collective-permute-done.2.kv_ref
  25.9 2.0 %tiles_2.1 = (f32[4,128,1024]{2,1,0:T(8,128)S(1)}, bf16[2,4,128,128]{3,2,1,0:T(8,128)(2,1)S(1)}) custom-call(s32[5,1,1024]{2,1,0:T(1,128)S(1)} %get-tuple-element.18.start_ref, f32[4,1,1024]{2,1,0:T(1,128)S(1)} %get-tuple-element.19.norm_ref, f32[4,1,1024]{2,1,0:T(1,128)S(1)} %get-tuple-element.20.delta_ref, ...), custom_call_target="tpu_custom_call", output_to_operand_aliasing={{0}: (6, {})} | custom-call | flops 671088640 | bytes 3145728 | tf_op jit(solution)/shard_map/tiles_2/pallas_call | solution.py:141
  27.9 9.7 %collective-permute-start.5 = (bf16[2,4,128,128]{3,2,1,0:T(8,128)(2,1)S(1)}, bf16[2,4,128,128]{3,2,1,0:T(8,128)(2,1)S(1)}, u32[]{:S(2)}, u32[]{:S(2)}) collective-permute-start(bf16[2,4,128,128]{3,2,1,0:T(8,128)(2,1)S(1)} %get-tuple-element.28), channel_id=1, source_target_pairs={{256,0},{320,64},{384,128},{448,192},{1,256},{65,320},{129,384},{1... | collective-permute-start | bytes 786440 | tf_op jit(solution)/shard_map/ppermute | solution.py:26
  37.6 0.0 collective-permute-done.1.kv_ref
  37.6 2.0 %tiles_3.1 = (f32[4,128,1024]{2,1,0:T(8,128)S(1)}, bf16[2,4,128,128]{3,2,1,0:T(8,128)(2,1)S(1)}) custom-call(s32[5,1,1024]{2,1,0:T(1,128)S(1)} %get-tuple-element.18.start_ref, f32[4,1,1024]{2,1,0:T(1,128)S(1)} %get-tuple-element.19.norm_ref, f32[4,1,1024]{2,1,0:T(1,128)S(1)} %get-tuple-element.20.delta_ref, ...), custom_call_target="tpu_custom_call", output_to_operand_aliasing={{0}: (6, {})} | custom-call | flops 671088640 | bytes 3145728 | tf_op jit(solution)/shard_map/tiles_3/pallas_call | solution.py:141
  39.6 4.6 %collective-permute-start.6 = (bf16[2,4,128,128]{3,2,1,0:T(8,128)(2,1)S(1)}, bf16[2,4,128,128]{3,2,1,0:T(8,128)(2,1)S(1)}, u32[]{:S(2)}, u32[]{:S(2)}) collective-permute-start(bf16[2,4,128,128]{3,2,1,0:T(8,128)(2,1)S(1)} %get-tuple-element.29), channel_id=1, source_target_pairs={{128,0},{192,64},{256,128},{320,192},{384,256},{448,320},{1,384},{... | collective-permute-start | bytes 786440 | tf_op jit(solution)/shard_map/ppermute | solution.py:26
  44.2 0.0 collective-permute-done.kv_ref
  44.2 2.0 %tiles_4.1 = (f32[4,128,1024]{2,1,0:T(8,128)S(1)}, bf16[2,4,128,128]{3,2,1,0:T(8,128)(2,1)S(1)}) custom-call(s32[5,1,1024]{2,1,0:T(1,128)S(1)} %get-tuple-element.18.start_ref, f32[4,1,1024]{2,1,0:T(1,128)S(1)} %get-tuple-element.19.norm_ref, f32[4,1,1024]{2,1,0:T(1,128)S(1)} %get-tuple-element.20.delta_ref, ...), custom_call_target="tpu_custom_call", output_to_operand_aliasing={{0}: (6, {})} | custom-call | flops 671088640 | bytes 3145728 | tf_op jit(solution)/shard_map/tiles_4/pallas_call | solution.py:141
  46.2 2.1 %collective-permute-start.7 = (bf16[2,4,128,128]{3,2,1,0:T(8,128)(2,1)S(1)}, bf16[2,4,128,128]{3,2,1,0:T(8,128)(2,1)S(1)}, u32[]{:S(2)}, u32[]{:S(2)}) collective-permute-start(bf16[2,4,128,128]{3,2,1,0:T(8,128)(2,1)S(1)} %get-tuple-element.30), channel_id=1, source_target_pairs={{64,0},{128,64},{192,128},{256,192},{320,256},{384,320},{448,384},... | collective-permute-start | bytes 786440 | tf_op jit(solution)/shard_map/ppermute | solution.py:26
  48.3 2.1 %tiles_0.1 = (f32[4,128,1024]{2,1,0:T(8,128)S(1)}, f32[2,4,128,128]{3,2,1,0:T(8,128)S(1)}) custom-call(s32[5,1,1024]{2,1,0:T(1,128)S(1)} %get-tuple-element.18.start_ref, f32[4,1,1024]{2,1,0:T(1,128)S(1)} %get-tuple-element.19.norm_ref, f32[4,1,1024]{2,1,0:T(1,128)S(1)} %get-tuple-element.20.delta_ref, ...), custom_call_target="tpu_custom_call", output_to_operand_aliasing={{0}: (6, {})} | custom-call | flops 671088640 | bytes 3145728 | tf_op jit(solution)/shard_map/tiles_0/pallas_call | solution.py:141
  50.3 0.8 %query_rows.1 = bf16[4,8,128,128]{3,2,1,0:T(8,128)(2,1)S(1)} custom-call(f32[4,128,1024]{2,1,0:T(8,128)S(1)} %get-tuple-element.25.total_ref), custom_call_target="tpu_custom_call" | custom-call | flops 524288 | bytes 3145728 | tf_op jit(solution)/shard_map/query_rows/pallas_call | solution.py:175
  51.2 1.6 %copy.26 = bf16[32,128,128]{2,0,1:T(8,128)(2,1)} copy(bf16[32,128,128]{2,1,0:T(8,128)(2,1)S(1)} %bitcast.26) | data formatting | bytes 2097152 | tf_op jit(solution)/shard_map/reshape | solution.py:255
  52.8 0.0 collective-permute-done.4.part_ref
  52.8 0.1 kv_sum.3.total_ref
  52.9 0.0 collective-permute-done.5.part_ref
  52.9 0.1 kv_sum.4.total_ref
  53.0 0.0 collective-permute-done.6.part_ref
  53.0 0.1 kv_sum.5.total_ref
  53.1 1.5 %collective-permute-done.7.part_ref = bf16[2,4,128,128]{3,2,1,0:T(8,128)(2,1)S(1)} collective-permute-done((bf16[2,4,128,128]{3,2,1,0:T(8,128)(2,1)S(1)}, bf16[2,4,128,128]{3,2,1,0:T(8,128)(2,1)S(1)}, u32[]{:S(2)}, u32[]{:S(2)}) %collective-permute-start.7) | collective-permute-done | bytes 262176 | tf_op jit(solution)/shard_map/ppermute | solution.py:26
  54.6 0.8 %kv_rows.1 = (bf16[128,4,128]{2,1,0:T(4,128)(2,1)}, bf16[128,4,128]{2,1,0:T(4,128)(2,1)}) custom-call(f32[2,4,128,128]{3,2,1,0:T(8,128)S(1)} %kv_sum.5.total_ref, bf16[2,4,128,128]{3,2,1,0:T(8,128)(2,1)S(1)} %collective-permute-done.7.part_ref), custom_call_target="tpu_custom_call" | custom-call | flops 131072 | bytes 1048576 | tf_op jit(solution)/shard_map/kv_rows/pallas_call | solution.py:216
  (1 shorter events, 0.0 us)
Async XLA Ops:
  1.7 17.7 %collective-permute-start.3 = (bf16[2,4,128,128]{3,2,1,0:T(8,128)(2,1)S(1)}, bf16[2,4,128,128]{3,2,1,0:T(8,128)(2,1)S(1)}, u32[]{:S(2)}, u32[]{:S(2)}) collective-permute-start(bf16[2,4,128,128]{3,2,1,0:T(8,128)(2,1)S(1)} %kv_stack.1.kv_ref), channel_id=1, source_target_pairs={{0,192},{64,256},{128,320},{192,384},{256,448},{320,1},{384,65},{4... | collective-permute-start | bytes 786440 | tf_op jit(solution)/shard_map/ppermute | solution.py:26
  5.8 20.1 %collective-permute-start.2 = (bf16[2,4,128,128]{3,2,1,0:T(8,128)(2,1)S(1)}, bf16[2,4,128,128]{3,2,1,0:T(8,128)(2,1)S(1)}, u32[]{:S(2)}, u32[]{:S(2)}) collective-permute-start(bf16[2,4,128,128]{3,2,1,0:T(8,128)(2,1)S(1)} %kv_stack.1.kv_ref), channel_id=1, source_target_pairs={{0,256},{64,320},{128,384},{192,448},{256,1},{320,65},{384,129},{4... | collective-permute-start | bytes 786440 | tf_op jit(solution)/shard_map/ppermute | solution.py:26
  10.2 27.4 %collective-permute-start.1 = (bf16[2,4,128,128]{3,2,1,0:T(8,128)(2,1)S(1)}, bf16[2,4,128,128]{3,2,1,0:T(8,128)(2,1)S(1)}, u32[]{:S(2)}, u32[]{:S(2)}) collective-permute-start(bf16[2,4,128,128]{3,2,1,0:T(8,128)(2,1)S(1)} %kv_stack.1.kv_ref), channel_id=1, source_target_pairs={{0,128},{64,192},{128,256},{192,320},{256,384},{320,448},{384,1},{... | collective-permute-start | bytes 786440 | tf_op jit(solution)/shard_map/ppermute | solution.py:26
  14.3 29.9 %collective-permute-start = (bf16[2,4,128,128]{3,2,1,0:T(8,128)(2,1)S(1)}, bf16[2,4,128,128]{3,2,1,0:T(8,128)(2,1)S(1)}, u32[]{:S(2)}, u32[]{:S(2)}) collective-permute-start(bf16[2,4,128,128]{3,2,1,0:T(8,128)(2,1)S(1)} %kv_stack.1.kv_ref), channel_id=1, source_target_pairs={{0,64},{64,128},{128,192},{192,256},{256,320},{320,384},{384,448},... | collective-permute-start | bytes 786440 | tf_op jit(solution)/shard_map/ppermute | solution.py:26
  16.4 1.8 %copy-start.3 = (bf16[128,32,128]{2,1,0:T(8,128)(2,1)S(1)}, bf16[128,32,128]{2,1,0:T(8,128)(2,1)}, u32[]{:S(2)}) copy-start(bf16[128,32,128]{2,1,0:T(8,128)(2,1)} %param.11) | copy-start | bytes 3145732
  16.4 2.2 %copy-start.4 = (s32[5]{0:T(128)S(1)}, s32[5]{0:T(128)}, u32[]{:S(2)}) copy-start(s32[5]{0:T(128)} %constant.23) | copy-start | bytes 64
  16.4 2.3 %copy-start = (f32[128,32]{0,1:T(8,128)S(1)}, f32[128,32]{0,1:T(8,128)}, u32[]{:S(2)}) copy-start(f32[128,32]{0,1:T(8,128)} %param.12) | copy-start | bytes 49156
  16.4 2.3 %copy-start.1 = (f32[128,32]{0,1:T(8,128)S(1)}, f32[128,32]{0,1:T(8,128)}, u32[]{:S(2)}) copy-start(f32[128,32]{0,1:T(8,128)} %param.13) | copy-start | bytes 49156
  16.4 2.3 %copy-start.2 = (s32[256]{0:T(256)S(1)}, s32[256]{0:T(256)}, u32[]{:S(2)}) copy-start(s32[256]{0:T(256)} %param.14) | copy-start | bytes 3076
  21.1 31.7 %collective-permute-start.4 = (bf16[2,4,128,128]{3,2,1,0:T(8,128)(2,1)S(1)}, bf16[2,4,128,128]{3,2,1,0:T(8,128)(2,1)S(1)}, u32[]{:S(2)}, u32[]{:S(2)}) collective-permute-start(bf16[2,4,128,128]{3,2,1,0:T(8,128)(2,1)S(1)} %get-tuple-element.27), channel_id=1, source_target_pairs={{192,0},{256,64},{320,128},{384,192},{448,256},{1,320},{65,384},{1... | collective-permute-start | bytes 786440 | tf_op jit(solution)/shard_map/ppermute | solution.py:26
  27.9 25.0 %collective-permute-start.5 = (bf16[2,4,128,128]{3,2,1,0:T(8,128)(2,1)S(1)}, bf16[2,4,128,128]{3,2,1,0:T(8,128)(2,1)S(1)}, u32[]{:S(2)}, u32[]{:S(2)}) collective-permute-start(bf16[2,4,128,128]{3,2,1,0:T(8,128)(2,1)S(1)} %get-tuple-element.28), channel_id=1, source_target_pairs={{256,0},{320,64},{384,128},{448,192},{1,256},{65,320},{129,384},{1... | collective-permute-start | bytes 786440 | tf_op jit(solution)/shard_map/ppermute | solution.py:26
  39.6 13.5 %collective-permute-start.6 = (bf16[2,4,128,128]{3,2,1,0:T(8,128)(2,1)S(1)}, bf16[2,4,128,128]{3,2,1,0:T(8,128)(2,1)S(1)}, u32[]{:S(2)}, u32[]{:S(2)}) collective-permute-start(bf16[2,4,128,128]{3,2,1,0:T(8,128)(2,1)S(1)} %get-tuple-element.29), channel_id=1, source_target_pairs={{128,0},{192,64},{256,128},{320,192},{384,256},{448,320},{1,384},{... | collective-permute-start | bytes 786440 | tf_op jit(solution)/shard_map/ppermute | solution.py:26
  46.2 8.5 %collective-permute-start.7 = (bf16[2,4,128,128]{3,2,1,0:T(8,128)(2,1)S(1)}, bf16[2,4,128,128]{3,2,1,0:T(8,128)(2,1)S(1)}, u32[]{:S(2)}, u32[]{:S(2)}) collective-permute-start(bf16[2,4,128,128]{3,2,1,0:T(8,128)(2,1)S(1)} %get-tuple-element.30), channel_id=1, source_target_pairs={{64,0},{128,64},{192,128},{256,192},{320,256},{384,320},{448,384},... | collective-permute-start | bytes 786440 | tf_op jit(solution)/shard_map/ppermute | solution.py:26
